TPU v7x, 128 devices: a whole 4x4x4 slice. The times are simulated.
128 devices in a mesh: section: 2 (over core), dp: 64 (over x, y, z).
Axes of the slice: x: 4, y: 4, z: 4, core: 2. Of those that a mesh axis runs over, the one named last changes fastest.
Arguments:
- tokens: bfloat16 [16384, 768], P('dp'), may hold values from -6 to 6
- lengths: int32 [256, 4], P('dp'), may hold values from 1 to 32, 64 in all within a row
- w_qkv: float32 [2, 768, 576], P('section', 'dp'), may hold values from -0.4375 to 0.4375
- b_qv: float32 [2, 1536], P('section', 'dp'), may hold values from -3 to 3
- w_post: float32 [2, 768, 768], P('section', 'dp'), may hold values from -0.625 to 0.625
- b_post: float32 [2, 768], P('section', 'dp'), may hold values from -3 to 3
- gain_one: float32 [2, 768], P('section', 'dp'), may hold values from 0.25 to 1.75
- shift_one: float32 [2, 768], P('section', 'dp'), may hold values from -3 to 3
- w_inter: float32 [2, 768, 768], P('section', 'dp'), may hold values from -0.4375 to 0.4375
- b_inter: float32 [2, 3072], P('section', 'dp'), may hold values from -3 to 3
- w_out: float32 [2, 3072, 192], P('section', 'dp'), may hold values from -0.21875 to 0.21875
- b_out: float32 [2, 768], P('section', 'dp'), may hold values from -3 to 3
- gain_two: float32 [2, 768], P('section', 'dp'), may hold values from 0.25 to 1.75
- shift_two: float32 [2, 768], P('section', 'dp'), may hold values from -3 to 3
- embed_table: float32 [768, 30528], P('dp', 'section'), may hold values from -0.21875 to 0.21875
- logit_grad: bfloat16 [16384, 30528], P('dp', 'section'), may hold values from -1 to 1
Outputs:
- logits: bfloat16 [16384, 30528], P('dp', 'section')
- token_grad: bfloat16 [16384, 768], P('dp', 'section')
- grad_w_qkv: float32 [2, 768, 576], P('section', 'dp')
- grad_b_qv: float32 [2, 1536], P('section', 'dp')
- grad_w_post: float32 [2, 768, 768], P('section', 'dp')
- grad_b_post: float32 [2, 768], P('section', 'dp')
- grad_gain_one: float32 [2, 768], P('section', 'dp')
- grad_shift_one: float32 [2, 768], P('section', 'dp')
- grad_w_inter: float32 [2, 768, 768], P('section', 'dp')
- grad_b_inter: float32 [2, 3072], P('section', 'dp')
- grad_w_out: float32 [2, 3072, 192], P('section', 'dp')
- grad_b_out: float32 [2, 768], P('section', 'dp')
- grad_gain_two: float32 [2, 768], P('section', 'dp')
- grad_shift_two: float32 [2, 768], P('section', 'dp')
- table_grad: float32 [768, 30528], P('dp', 'section')
Inputs may be any that keep to these rules, and one draw needn't show every extreme that they name: Each row holds the lengths of 4 sequences packed in order into one micro-batch, summing to 64; the longest is 32.
All inputs are finite; a program needn't handle non-finite values.
Results may differ from a plain program's by a relative error of at most 0.022.
Values may be sent and summed in bfloat16 or wider, within the bound.
No kernel may reach another device: no remote copies, remote signals or barrier semaphores. Data moves between devices by JAX's collectives and lax.ppermute only.
A program may use at most 384 MiB of HBM per device.

v0:
```python
import jax
import jax.numpy as jnp
from jax import lax
from jax.sharding import PartitionSpec as P


def shifted(block, axis, distance):
    devices = range(lax.axis_size(axis))
    route = [(i - distance, i) for i in devices if i - distance in devices]
    return lax.ppermute(block, axis, route)


def layer_norm(values, gain, shift):
    row_mean = jnp.mean(values, axis=-1, keepdims=True)
    centred = values - row_mean
    variance = jnp.mean(centred * centred, axis=-1, keepdims=True)
    return centred * lax.rsqrt(variance + 1e-12) * gain + shift


def gelu_exact(values):
    return jax.nn.gelu(values, approximate=False)


def same_document(length_row, row_count):
    doc_ends = jnp.cumsum(length_row)
    places = jnp.arange(row_count, dtype=jnp.int32)
    doc_index = jnp.sum((places[:, None] >= doc_ends[None, :]).astype(jnp.int32), axis=1)
    return doc_index[:, None] == doc_index[None, :]


def grouped(values, matrix):
    row_count = values.shape[0]
    fan_in = matrix.shape[0] // 4
    return jnp.einsum(
        "ngc,gcf->ngf",
        values.reshape(row_count, 4, fan_in),
        matrix.reshape(4, fan_in, matrix.shape[1]),
        preferred_element_type=jnp.float32,
    )


def make_table_term(head_rows, grad_columns):
    return jnp.einsum("nc,nv->cv", head_rows, grad_columns, preferred_element_type=jnp.float32)


def layer_forward(inputs, doc_mask, weights):
    (
        w_qkv,
        b_qv,
        w_post,
        b_post,
        gain_one,
        shift_one,
        w_inter,
        b_inter,
        w_out,
        b_out,
        gain_two,
        shift_two,
    ) = weights
    row_count, model_width = inputs.shape
    group_width = model_width // 4
    head_count = model_width // 64
    project = grouped(inputs, w_qkv)
    bias_float = b_qv.astype(jnp.float32)
    queries = (
        project[:, :, :group_width].reshape(row_count, model_width) + bias_float[:model_width]
    ).astype(jnp.bfloat16)
    keys_part = (
        project[:, :, group_width : 2 * group_width]
        .reshape(row_count, model_width)
        .astype(jnp.bfloat16)
    )
    values_part = (
        project[:, :, 2 * group_width :].reshape(row_count, model_width) + bias_float[model_width:]
    ).astype(jnp.bfloat16)
    query_heads = queries.reshape(row_count, head_count, 64)
    key_heads = keys_part.reshape(row_count, head_count, 64)
    value_heads = values_part.reshape(row_count, head_count, 64)
    scores = (
        jnp.einsum("qhd,khd->hqk", query_heads, key_heads, preferred_element_type=jnp.float32)
        * 0.125
    )
    scores = jnp.where(doc_mask[None], scores, -1e30)
    row_top = jnp.max(scores, axis=-1, keepdims=True)
    exponents = jnp.exp(scores - row_top)
    row_total = jnp.sum(exponents, axis=-1, keepdims=True)
    attention = (exponents / row_total).astype(jnp.bfloat16)
    log_total = row_top + jnp.log(row_total)
    context = (
        jnp.einsum("hqk,khd->qhd", attention, value_heads, preferred_element_type=jnp.float32)
        .reshape(row_count, model_width)
        .astype(jnp.bfloat16)
    )
    post_out = jnp.dot(context, w_post, preferred_element_type=jnp.float32) + b_post.astype(
        jnp.float32
    )
    resid_one = post_out + inputs.astype(jnp.float32)
    hidden = layer_norm(
        resid_one, gain_one.astype(jnp.float32), shift_one.astype(jnp.float32)
    ).astype(jnp.bfloat16)
    inter_pre = grouped(hidden, w_inter).reshape(row_count, -1) + b_inter.astype(jnp.float32)
    activated = gelu_exact(inter_pre).astype(jnp.bfloat16)
    output = grouped(activated, w_out).reshape(row_count, model_width) + b_out.astype(jnp.float32)
    resid_two = output + hidden.astype(jnp.float32)
    result = layer_norm(
        resid_two, gain_two.astype(jnp.float32), shift_two.astype(jnp.float32)
    ).astype(jnp.bfloat16)
    kept = (
        inputs,
        queries,
        keys_part,
        values_part,
        log_total,
        context,
        resid_one,
        hidden,
        inter_pre,
        activated,
        resid_two,
    )
    return (result, kept)


def layer_backward(grad_out, kept, doc_mask, weights):
    (
        w_qkv,
        b_qv,
        w_post,
        b_post,
        gain_one,
        shift_one,
        w_inter,
        b_inter,
        w_out,
        b_out,
        gain_two,
        shift_two,
    ) = weights
    (
        inputs,
        queries,
        keys_part,
        values_part,
        log_total,
        context,
        resid_one,
        hidden,
        inter_pre,
        activated,
        resid_two,
    ) = kept
    row_count, model_width = inputs.shape
    group_width = model_width // 4
    head_count = model_width // 64
    inter_width = inter_pre.shape[1] // 4
    norm_value, norm_two_back = jax.vjp(
        layer_norm, resid_two, gain_two.astype(jnp.float32), shift_two.astype(jnp.float32)
    )
    grad_resid_two, grad_gain_two, grad_shift_two = norm_two_back(grad_out)
    grad_output = grad_resid_two.astype(jnp.bfloat16)
    grad_b_out = jnp.sum(grad_output, axis=0, dtype=jnp.float32)
    output_groups = grad_output.reshape(row_count, 4, group_width)
    grad_w_out = jnp.einsum(
        "ngc,ngf->gcf",
        activated.reshape(row_count, 4, inter_width),
        output_groups,
        preferred_element_type=jnp.float32,
    ).reshape(4 * inter_width, group_width)
    grad_activated = jnp.einsum(
        "ngf,gcf->ngc",
        output_groups,
        w_out.reshape(4, inter_width, group_width),
        preferred_element_type=jnp.float32,
    ).reshape(row_count, 4 * inter_width)
    gelu_value, gelu_back = jax.vjp(gelu_exact, inter_pre)
    grad_inter = gelu_back(grad_activated)[0].astype(jnp.bfloat16)
    grad_b_inter = jnp.sum(grad_inter, axis=0, dtype=jnp.float32)
    inter_groups = grad_inter.reshape(row_count, 4, inter_width)
    grad_w_inter = jnp.einsum(
        "ngc,ngf->gcf",
        hidden.reshape(row_count, 4, group_width),
        inter_groups,
        preferred_element_type=jnp.float32,
    ).reshape(model_width, inter_width)
    grad_hidden = (
        grad_resid_two
        + jnp.einsum(
            "ngf,gcf->ngc",
            inter_groups,
            w_inter.reshape(4, group_width, inter_width),
            preferred_element_type=jnp.float32,
        ).reshape(row_count, model_width)
    ).astype(jnp.bfloat16)
    norm_value, norm_one_back = jax.vjp(
        layer_norm, resid_one, gain_one.astype(jnp.float32), shift_one.astype(jnp.float32)
    )
    grad_resid_one, grad_gain_one, grad_shift_one = norm_one_back(grad_hidden.astype(jnp.float32))
    grad_post = grad_resid_one.astype(jnp.bfloat16)
    grad_b_post = jnp.sum(grad_post, axis=0, dtype=jnp.float32)
    grad_w_post = jnp.einsum("nc,nf->cf", context, grad_post, preferred_element_type=jnp.float32)
    grad_context = jnp.einsum(
        "nf,cf->nc", grad_post, w_post, preferred_element_type=jnp.float32
    ).astype(jnp.bfloat16)
    query_heads = queries.reshape(row_count, head_count, 64)
    key_heads = keys_part.reshape(row_count, head_count, 64)
    value_heads = values_part.reshape(row_count, head_count, 64)
    context_heads = grad_context.reshape(row_count, head_count, 64)
    scores = (
        jnp.einsum("qhd,khd->hqk", query_heads, key_heads, preferred_element_type=jnp.float32)
        * 0.125
    )
    scores = jnp.where(doc_mask[None], scores, -1e30)
    attention = jnp.exp(scores - log_total)
    grad_attention = jnp.einsum(
        "qhd,khd->hqk", context_heads, value_heads, preferred_element_type=jnp.float32
    )
    grad_values = (
        jnp.einsum(
            "hqk,qhd->khd",
            attention.astype(jnp.bfloat16),
            context_heads,
            preferred_element_type=jnp.float32,
        )
        .reshape(row_count, model_width)
        .astype(jnp.bfloat16)
    )
    row_inner = jnp.sum(attention * grad_attention, axis=-1, keepdims=True)
    grad_scores = (attention * (grad_attention - row_inner)).astype(jnp.bfloat16)
    grad_queries = (
        (
            jnp.einsum("hqk,khd->qhd", grad_scores, key_heads, preferred_element_type=jnp.float32)
            * 0.125
        )
        .reshape(row_count, model_width)
        .astype(jnp.bfloat16)
    )
    grad_keys = (
        (
            jnp.einsum("hqk,qhd->khd", grad_scores, query_heads, preferred_element_type=jnp.float32)
            * 0.125
        )
        .reshape(row_count, model_width)
        .astype(jnp.bfloat16)
    )
    grad_b_qv = jnp.concatenate(
        [
            jnp.sum(grad_queries, axis=0, dtype=jnp.float32),
            jnp.sum(grad_values, axis=0, dtype=jnp.float32),
        ]
    )
    grad_project = jnp.concatenate(
        [
            grad_queries.reshape(row_count, 4, group_width),
            grad_keys.reshape(row_count, 4, group_width),
            grad_values.reshape(row_count, 4, group_width),
        ],
        axis=2,
    )
    grad_w_qkv = jnp.einsum(
        "ngc,ngf->gcf",
        inputs.reshape(row_count, 4, group_width),
        grad_project,
        preferred_element_type=jnp.float32,
    ).reshape(model_width, 3 * group_width)
    grad_inputs = grad_resid_one + jnp.einsum(
        "ngf,gcf->ngc",
        grad_project,
        w_qkv.reshape(4, group_width, 3 * group_width),
        preferred_element_type=jnp.float32,
    ).reshape(row_count, model_width)
    return (
        grad_inputs,
        (
            grad_w_qkv,
            grad_b_qv,
            grad_w_post,
            grad_b_post,
            grad_gain_one,
            grad_shift_one,
            grad_w_inter,
            grad_b_inter,
            grad_w_out,
            grad_b_out,
            grad_gain_two,
            grad_shift_two,
        ),
    )


def per_device(
    tokens,
    lengths,
    w_qkv,
    b_qv,
    w_post,
    b_post,
    gain_one,
    shift_one,
    w_inter,
    b_inter,
    w_out,
    b_out,
    gain_two,
    shift_two,
    embed_table,
    logit_grad,
):
    shards = (
        w_qkv[0].astype(jnp.bfloat16),
        b_qv[0].astype(jnp.bfloat16),
        w_post[0].astype(jnp.bfloat16),
        b_post[0].astype(jnp.bfloat16),
        gain_one[0].astype(jnp.bfloat16),
        shift_one[0].astype(jnp.bfloat16),
        w_inter[0].astype(jnp.bfloat16),
        b_inter[0].astype(jnp.bfloat16),
        w_out[0].astype(jnp.bfloat16),
        b_out[0].astype(jnp.bfloat16),
        gain_two[0].astype(jnp.bfloat16),
        shift_two[0].astype(jnp.bfloat16),
    )
    gathered = (
        lax.all_gather(shards[0], "dp", axis=0, tiled=True),
        lax.all_gather(shards[1], "dp", axis=0, tiled=True),
        lax.all_gather(shards[2], "dp", axis=0, tiled=True),
        lax.all_gather(shards[3], "dp", axis=0, tiled=True),
        lax.all_gather(shards[4], "dp", axis=0, tiled=True),
        lax.all_gather(shards[5], "dp", axis=0, tiled=True),
        lax.all_gather(shards[6], "dp", axis=0, tiled=True),
        lax.all_gather(shards[7], "dp", axis=0, tiled=True),
        lax.all_gather(shards[8], "dp", axis=0, tiled=True),
        lax.all_gather(shards[9], "dp", axis=0, tiled=True),
        lax.all_gather(shards[10], "dp", axis=0, tiled=True),
        lax.all_gather(shards[11], "dp", axis=0, tiled=True),
    )
    section_index = lax.axis_index("section")
    is_first = section_index == 0
    micro_count = lengths.shape[0]
    micro_rows = tokens.shape[0] // micro_count
    model_width = tokens.shape[1]
    masks = [same_document(lengths[number], micro_rows) for number in range(micro_count)]
    received = jnp.zeros((micro_rows, model_width), jnp.bfloat16)
    stored = []
    finals = []
    for step_index in range(micro_count + 1):
        first_micro = min(step_index, micro_count - 1)
        second_micro = max(step_index - 1, 0)
        own_rows = tokens[first_micro * micro_rows : (first_micro + 1) * micro_rows]
        current = jnp.where(is_first, own_rows, received)
        doc_mask = jnp.where(is_first, masks[first_micro], masks[second_micro])
        result, kept = layer_forward(current, doc_mask, gathered)
        stored.append((kept, doc_mask))
        if step_index >= 1:
            finals.append(result)
        if step_index < micro_count:
            received = shifted(result, "section", 1)
    last_rows = jnp.concatenate(finals, axis=0)
    other_rows = shifted(last_rows, "section", -1)
    head_rows = jnp.where(is_first, other_rows, last_rows)
    table_low = embed_table.astype(jnp.bfloat16)
    logit_sums = jnp.dot(
        head_rows,
        lax.all_gather(table_low, "dp", axis=0, tiled=True),
        preferred_element_type=jnp.float32,
    )
    head_part = jnp.einsum(
        "nv,cv->nc",
        logit_grad,
        lax.all_gather(table_low, "dp", axis=0, tiled=True),
        preferred_element_type=jnp.float32,
    )
    grad_top = lax.psum(head_part, "section")
    table_grad = lax.psum_scatter(
        make_table_term(head_rows, logit_grad), "dp", scatter_dimension=0, tiled=True
    )
    grad_sums = tuple((jnp.zeros(weight.shape, jnp.float32) for weight in gathered))
    grad_received = jnp.zeros((micro_rows, model_width), jnp.bfloat16)
    input_blocks = []
    for step_index in range(micro_count + 1):
        kept, doc_mask = stored[micro_count - step_index]
        second_micro = max(micro_count - 1 - step_index, 0)
        own_grad = grad_top[second_micro * micro_rows : (second_micro + 1) * micro_rows]
        current = jnp.where(is_first, grad_received.astype(jnp.float32), own_grad)
        grad_inputs, weight_terms = layer_backward(current, kept, doc_mask, gathered)
        is_valid = jnp.where(is_first, step_index >= 1, step_index < micro_count)

        def add_term(running, term_value):
            return running + jnp.where(is_valid, term_value, 0.0)

        grad_sums = jax.tree.map(add_term, grad_sums, weight_terms)
        if step_index >= 1:
            input_blocks.append(grad_inputs)
        if step_index < micro_count:
            grad_received = shifted(grad_inputs.astype(jnp.bfloat16), "section", -1)
    token_full = jnp.concatenate(input_blocks[::-1], axis=0).astype(jnp.bfloat16)
    half_width = model_width // 2
    upper_half = shifted(token_full[:, half_width:], "section", 1)
    token_out = jnp.where(is_first, token_full[:, :half_width], upper_half)
    scattered = lax.psum_scatter(grad_sums, "dp", scatter_dimension=0, tiled=True)
    return (
        (logit_sums.astype(jnp.bfloat16), token_out)
        + tuple((scattered_part[None] for scattered_part in scattered))
        + (table_grad,)
    )


def solution(mesh):
    return jax.shard_map(
        per_device,
        mesh=mesh,
        in_specs=(
            P("dp", None),
            P("dp", None),
            P("section", "dp", None),
            P("section", "dp"),
            P("section", "dp", None),
            P("section", "dp"),
            P("section", "dp"),
            P("section", "dp"),
            P("section", "dp", None),
            P("section", "dp"),
            P("section", "dp", None),
            P("section", "dp"),
            P("section", "dp"),
            P("section", "dp"),
            P("dp", "section"),
            P("dp", "section"),
        ),
        out_specs=(
            P("dp", "section"),
            P("dp", "section"),
            P("section", "dp", None),
            P("section", "dp"),
            P("section", "dp", None),
            P("section", "dp"),
            P("section", "dp"),
            P("section", "dp"),
            P("section", "dp", None),
            P("section", "dp"),
            P("section", "dp", None),
            P("section", "dp"),
            P("section", "dp"),
            P("section", "dp"),
            P("dp", "section"),
        ),
        check_vma=False,
    )
```

profile of v0, /device:TPU:0, one launch (start us, length us, event | category | flops | bytes accessed | tf_op | source)
XLA Modules:
  0.0 1811.0 jit_solution(13250037051557939335)
XLA Ops:
  19.2 352.8 %all-reduce.24 = (bf16[1536]{0:T(1024)(128)(2,1)S(1)}, bf16[3072]{0:T(1024)(128)(2,1)S(1)}, bf16[768]{0:T(1024)(128)(2,1)S(1)}, bf16[768]{0:T(1024)(128)(2,1)S(1...) all-reduce(bf16[1536]{0:T(1024)(128)(2,1)S(1)} %dynamic-update-slic, ...), channel_id=3, replica_groups=mesh['section'=2,'dp'=64] {'dp'}, use_global_device_ids=true, to_apply=%add | all-reduce | flops 9216 | bytes 36864
  375.1 180.1 %all-gather = bf16[1,768,576]{2,0,1:T(2,128)(2,1)S(1)} all-gather(bf16[1,12,576]{2,0,1:T(2,128)(2,1)S(1)} %convert_element_type.787), channel_id=2, replica_groups=mesh['section'=2,'dp'=64] {'dp'}, dimensions={1}, use_global_device_ids=true | all-gather | bytes 898560 | tf_op jit(solution)/shard_map/all_gather | solution.py:324
  564.2 3.8 fusion.114
  596.9 4.0 fusion.106
  631.9 4.0 fusion.98
  668.0 4.0 fusion.90
  702.8 4.1 fusion.82
  712.8 34.2 %reshape.1328 = bf16[768,15264]{1,0:T(8,128)(2,1)} reshape(bf16[64,12,15264]{2,1,0:T(8,128)(2,1)} %all-gather.24.cloned.1.call-done) | data formatting | bytes 46891008
  747.0 14.2 fusion.366
  766.2 15.0 all-reduce.29.cloned.1.call-done
  789.2 3.2 convert_reduce_fusion.4
  838.1 3.1 convert_reduce_fusion.3
  878.1 2.9 fusion.259
  885.7 3.1 convert_reduce_fusion.2
  925.4 2.9 fusion.256
  933.1 3.1 convert_reduce_fusion.1
  978.7 4.7 select_add_fusion
  983.4 3.4 copy.791
  992.5 20.6 %fusion.231 = f32[768,15264]{1,0:T(8,128)} fusion(bf16[256,15264]{0,1:T(8,128)(2,1)} %param.31, bf16[256,768]{1,0:T(8,128)(2,1)} %collective-permute-done.4, pred[]{:T(512)S(6)} %eq.83, bf16[64,768]{1,0:T(8,128)(2,1)S(1)} %copy-done.113, bf16[64,768]{1,0:T(8,128)(2,1)} %copy-done.118, bf16[64,768]{1,0:T(8,128)(2,1)S(1)} %copy-done.116, ...), kind=kOutput, calls=%fused_computation.465 | convolution fusion | flops 6003818496 | bytes 55492608 | tf_op jit(solution)/shard_map/nc,nv->cv/dot_general | solution.py:43
  1043.2 15.7 convolution_convert_fusion
  1082.9 228.0 %fusion.329 = (f32[16,576]{1,0:T(8,128)S(1)}, f32[16,768]{1,0:T(8,128)S(1)}, f32[16,768]{1,0:T(8,128)S(1)}) fusion(f32[768,576]{1,0:T(8,128)} %bitcast.748, f32[768,768]{1,0:T(8,128)} %select_add_fusion.2, f32[768,768]{1,0:T(8,128)} %bitcast.747), kind=kCustom, calls=%all-reduce-scatter.3 | all-reduce-scatter fusion | flops 2162689 | bytes 6623744
  1320.8 347.8 %all-reduce.23 = (f32[1536]{0:T(1024)S(1)}, f32[768]{0:T(1024)S(1)}, f32[768]{0:T(1024)S(1)}, f32[768]{0:T(1024)S(1)}, f32[3072]{0:T(1024)S(1)}, /*index=5*/f32[...) all-reduce(f32[1536]{0:T(1024)S(1)} %fusion.304, ...), channel_id=15, replica_groups=mesh['section'=2,'dp'=64] {'dp'}, use_global_device_ids=true, to_apply=%region_75.76.clone | all-reduce | flops 9216 | bytes 73728
  1678.4 4.5 collective-permute-start.14
  1683.0 8.3 collective-permute-start.13
  1691.3 13.0 collective-permute-start.12
  1706.3 3.4 collective-permute-start.10
  1721.0 3.1 collective-permute-start.36
  1734.8 3.4 collective-permute-start.31
  1742.9 5.0 collective-permute-start.28
  1767.9 3.2 collective-permute-start.50
  1775.2 3.2 collective-permute-start.47
  1784.6 4.7 collective-permute-start.44
  (1075 shorter events, 481.2 us)
Async XLA Ops:
  7.3 551.3 %all-gather.18.cloned.1.call-start = ((), (), s32[]{:S(2)}) async-start(), calls=%async_computation.2 | async-start | bytes 2396160 | tf_op jit(solution)/shard_map/all_gather | solution.py:326
  8.8 553.5 %all-gather.20.cloned.1.call-start = ((), (), s32[]{:S(2)}) async-start(), calls=%async_computation.3 | async-start | bytes 2396160 | tf_op jit(solution)/shard_map/all_gather | solution.py:330
  10.3 557.7 %all-gather.22.cloned.1.call-start = ((), (), s32[]{:S(2)}) async-start(), calls=%async_computation.4 | async-start | bytes 1597440 | tf_op jit(solution)/shard_map/all_gather | solution.py:332
  11.8 701.1 %all-gather.24.cloned.1.call-start = ((), (), s32[]{:S(2)}) async-start(), calls=%async_computation.5 | async-start | bytes 31948800 | tf_op jit(solution)/shard_map/all_gather | solution.py:364
  13.9 767.3 %all-reduce.29.cloned.1.call-start = ((), (), s32[]{:S(2)}) async-start(), calls=%async_computation.1 | async-start | bytes 1572864 | tf_op jit(solution)/shard_map/psum | solution.py:373
  761.3 1038.7 %reduce-scatter.10.cloned.1.call-start = ((), (), s32[]{:S(2)}) async-start(), calls=%async_computation.6 | async-start | bytes 3194880
  986.8 814.7 %all-reduce.31.cloned.1.call-start = ((), (), s32[]{:S(2)}) async-start(), calls=%async_computation.7 | async-start | bytes 94371840
  1311.3 360.0 %collective-permute-start.24 = (f32[16,576]{1,0:T(8,128)S(1)}, f32[16,576]{1,0:T(8,128)S(1)}, u32[]{:S(2)}, u32[]{:S(2)}) collective-permute-start(f32[16,576]{1,0:T(8,128)S(1)} %get-tuple-element.141), channel_id=1, source_target_pairs={{0,15},{1,16},{2,17},{3,18},{4,19},{5,20},{6,21},{7,22},{8,23},{9,... | collective-permute-start | bytes 110600
  1312.7 359.9 %collective-permute-start.23 = (f32[16,576]{1,0:T(8,128)S(1)}, f32[16,576]{1,0:T(8,128)S(1)}, u32[]{:S(2)}, u32[]{:S(2)}) collective-permute-start(f32[16,576]{1,0:T(8,128)S(1)} %get-tuple-element.141), channel_id=1, source_target_pairs={{0,14},{1,15},{2,16},{3,17},{4,18},{5,19},{6,20},{7,21},{8,22},{9,... | collective-permute-start | bytes 110600
  1314.0 359.9 %collective-permute-start.22 = (f32[16,576]{1,0:T(8,128)S(1)}, f32[16,576]{1,0:T(8,128)S(1)}, u32[]{:S(2)}, u32[]{:S(2)}) collective-permute-start(f32[16,576]{1,0:T(8,128)S(1)} %get-tuple-element.141), channel_id=1, source_target_pairs={{0,13},{1,14},{2,15},{3,16},{4,17},{5,18},{6,19},{7,20},{8,21},{9,... | collective-permute-start | bytes 110600
  1315.3 360.5 %collective-permute-start.21 = (f32[16,576]{1,0:T(8,128)S(1)}, f32[16,576]{1,0:T(8,128)S(1)}, u32[]{:S(2)}, u32[]{:S(2)}) collective-permute-start(f32[16,576]{1,0:T(8,128)S(1)} %get-tuple-element.141), channel_id=1, source_target_pairs={{0,12},{1,13},{2,14},{3,15},{4,16},{5,17},{6,18},{7,19},{8,20},{9,... | collective-permute-start | bytes 110600
  1318.4 351.6 %collective-permute-start.25 = (f32[12,576]{1,0:T(8,128)S(1)}, f32[12,576]{1,0:T(8,128)S(1)}, u32[]{:S(2)}, u32[]{:S(2)}) collective-permute-start(f32[12,576]{1,0:T(8,128)S(1)} %slice.182), channel_id=1, source_target_pairs={{0,16},{1,17},{2,18},{3,19},{4,20},{5,21},{6,22},{7,23},{8,24},{9,... | collective-permute-start | bytes 82952
  1673.9 17.4 collective-permute-start.17
  1675.8 29.1 %collective-permute-start.16 = (f32[16,576]{1,0:T(8,128)S(1)}, f32[16,576]{1,0:T(8,128)S(1)}, u32[]{:S(2)}, u32[]{:S(2)}) collective-permute-start(f32[16,576]{1,0:T(8,128)S(1)} %get-tuple-element.141), channel_id=1, source_target_pairs={{0,7},{1,8},{2,9},{3,10},{4,11},{5,12},{6,13},{7,14},{8,15},{9,16}... | collective-permute-start | bytes 110600
  1677.1 29.1 %collective-permute-start.15 = (f32[16,576]{1,0:T(8,128)S(1)}, f32[16,576]{1,0:T(8,128)S(1)}, u32[]{:S(2)}, u32[]{:S(2)}) collective-permute-start(f32[16,576]{1,0:T(8,128)S(1)} %get-tuple-element.141), channel_id=1, source_target_pairs={{0,6},{1,7},{2,8},{3,9},{4,10},{5,11},{6,12},{7,13},{8,14},{9,15},... | collective-permute-start | bytes 110600
  1678.4 31.2 %collective-permute-start.14 = (f32[16,576]{1,0:T(8,128)S(1)}, f32[16,576]{1,0:T(8,128)S(1)}, u32[]{:S(2)}, u32[]{:S(2)}) collective-permute-start(f32[16,576]{1,0:T(8,128)S(1)} %get-tuple-element.141), channel_id=1, source_target_pairs={{0,5},{1,6},{2,7},{3,8},{4,9},{5,10},{6,11},{7,12},{8,13},{9,14},{... | collective-permute-start | bytes 110600
  1683.0 29.6 %collective-permute-start.13 = (f32[16,576]{1,0:T(8,128)S(1)}, f32[16,576]{1,0:T(8,128)S(1)}, u32[]{:S(2)}, u32[]{:S(2)}) collective-permute-start(f32[16,576]{1,0:T(8,128)S(1)} %get-tuple-element.141), channel_id=1, source_target_pairs={{0,4},{1,5},{2,6},{3,7},{4,8},{5,9},{6,10},{7,11},{8,12},{9,13},{1... | collective-permute-start | bytes 110600
  1691.3 22.5 %collective-permute-start.12 = (f32[16,576]{1,0:T(8,128)S(1)}, f32[16,576]{1,0:T(8,128)S(1)}, u32[]{:S(2)}, u32[]{:S(2)}) collective-permute-start(f32[16,576]{1,0:T(8,128)S(1)} %get-tuple-element.141), channel_id=1, source_target_pairs={{0,3},{1,4},{2,5},{3,6},{4,7},{5,8},{6,9},{7,10},{8,11},{9,12},{10... | collective-permute-start | bytes 110600
  1709.7 14.4 collective-permute-start.40
  1724.1 14.2 collective-permute-start.35
  1732.3 15.6 collective-permute-start.32
  1734.8 15.2 collective-permute-start.31
  1738.3 14.3 collective-permute-start.30
  1741.0 15.0 collective-permute-start.29
  1742.9 14.7 collective-permute-start.28
  1758.9 14.1 collective-permute-start.53
  1760.3 15.0 collective-permute-start.52
  1763.1 15.4 collective-permute-start.51
  1767.9 14.5 collective-permute-start.50
  1773.0 16.3 collective-permute-start.48
  1775.2 16.4 collective-permute-start.47
  1778.4 16.0 collective-permute-start.46
  (308 other events, 4566.6 us)
Sparse Core Ops, SparseCore 0:
  11.5 68.4 all-gather.17
  83.4 63.3 all-gather.19
  150.3 62.2 all-gather.21
  215.3 156.8 all-gather.23
  761.4 19.7 all-reduce.28
  986.9 228.9 reduce-scatter.9
  1222.8 449.5 all-reduce.30
where the time goes:
time: 1830 us; the launch traced here: 1810 us
  blocking collectives  1110 us (61%)
  local copies, waits for them, and re-layouts  240 us (13%)
  matrix products  193 us (11%)
  starting transfers between devices  139 us (8%)
  other arithmetic  87.6 us (5%)
  between operations  23.2 us (1%)
  waiting for transfers between devices  19.6 us (1%)
    unnamed x3, blocking collectives  928 us
    all_gather x1, blocking collectives, per_device(): lax.all_gather(shards[0], 'dp', axis=0, tiled=True)  180 us
    unnamed x50, starting transfers between devices  122 us
    unnamed x584, local copies, waits for them, and re-layouts  90.3 us
  transfers between devices with their start and end apart: 65, of which 5 were waited for; matrix products, arithmetic and copies ran while one was open for 27% of the time, Pallas kernels for 0%

commit v1 on v0

v1 whole, which is shorter than its diff:
```python
import functools
import jax
import jax.numpy as jnp
from jax import lax
from jax.experimental import pallas as pl
from jax.experimental.pallas import tpu as pltpu
from jax.sharding import PartitionSpec as P

BF = jnp.bfloat16
F32 = jnp.float32
ROWS, WIDTH, FF_GROUP, GROUP, HEADS = 128, 768, 768, 192, 12
SHARD = {
    "b_qv": (0, 24), "b_inter": (24, 48), "b_post": (72, 12), "gain_one": (84, 12),
    "shift_one": (96, 12), "b_out": (108, 12), "gain_two": (120, 12), "shift_two": (132, 12),
}
PLACE, _at = {}, 0
for _name, (_off, _width) in SHARD.items():
    PLACE[_name] = (_at, 64 * _width)
    _at += 64 * _width
VECTOR = _at


def dot(a, b):
    return lax.dot_general(a, b, (((1,), (0,)), ((), ())), preferred_element_type=F32)


def dot_nt(a, b):
    return lax.dot_general(a, b, (((1,), (1,)), ((), ())), preferred_element_type=F32)


def dot_tn(a, b):
    return lax.dot_general(a, b, (((0,), (0,)), ((), ())), preferred_element_type=F32)


def vector_of(vec_ref, name):
    at, size = PLACE[name]
    return vec_ref[:, at : at + size]


def norm_parts(values):
    mean = jnp.mean(values, axis=-1, keepdims=True)
    centred = values - mean
    scale = lax.rsqrt(jnp.mean(centred * centred, axis=-1, keepdims=True) + 1e-12)
    return centred * scale, scale


def same_doc(lengths_ref, first_row):
    row = lax.broadcasted_iota(jnp.int32, (ROWS, ROWS), 0)
    col = lax.broadcasted_iota(jnp.int32, (ROWS, ROWS), 1)
    row_id = jnp.zeros((ROWS, ROWS), jnp.int32)
    col_id = jnp.zeros((ROWS, ROWS), jnp.int32)
    for micro in range(2):
        end = micro * 64
        for doc in range(4):
            end = end + lengths_ref[first_row + micro, doc]
            row_id = row_id + (row >= end).astype(jnp.int32)
            col_id = col_id + (col >= end).astype(jnp.int32)
    return row_id == col_id


def gelu_parts(x):
    half = 0.5 * (1.0 + lax.erf(x * 0.7071067811865476))
    return half


def layer_forward(u_ref, same, wa, wb, wc, vec_ref, y_ref, q_ref, k_ref, v_ref, p_ref, ctx_ref, xh1_ref, rs1_ref, hid_ref, inter_ref, xh2_ref, rs2_ref):
    u = u_ref[...]
    for g in range(4):
        cols = slice(GROUP * g, GROUP * (g + 1))
        block = dot(u[:, cols], wa(g))
        b_q = vec_ref[:, PLACE["b_qv"][0] + GROUP * g : PLACE["b_qv"][0] + GROUP * (g + 1)]
        b_v = vec_ref[:, PLACE["b_qv"][0] + WIDTH + GROUP * g : PLACE["b_qv"][0] + WIDTH + GROUP * (g + 1)]
        q_ref[:, cols] = (block[:, :GROUP] + b_q).astype(BF)
        k_ref[:, cols] = block[:, GROUP : 2 * GROUP].astype(BF)
        v_ref[:, cols] = (block[:, 2 * GROUP : 3 * GROUP] + b_v).astype(BF)
    lane = lax.broadcasted_iota(jnp.int32, (ROWS, 128), 1)
    for pair in range(HEADS // 2):
        cols = slice(128 * pair, 128 * (pair + 1))
        qt, kt, vt = q_ref[:, cols], k_ref[:, cols], v_ref[:, cols]
        outs = []
        for half in range(2):
            mine = (lane >= 64) if half else (lane < 64)
            qm = jnp.where(mine, qt, jnp.zeros_like(qt))
            scores = jnp.where(same, dot_nt(qm, kt) * 0.125, -1e30)
            top = jnp.max(scores, axis=-1, keepdims=True)
            e = jnp.exp(scores - top)
            p = e / jnp.sum(e, axis=-1, keepdims=True)
            p_ref[2 * pair + half] = p
            outs.append(dot(p.astype(BF), vt))
        ctx_ref[:, cols] = jnp.where(lane < 64, outs[0], outs[1]).astype(BF)
    ctx = ctx_ref[...]
    w_post, _ = wb(None)
    r1 = dot(ctx, w_post) + vector_of(vec_ref, "b_post") + u.astype(F32)
    xh, rs = norm_parts(r1)
    xh1_ref[...] = xh
    rs1_ref[...] = jnp.broadcast_to(rs, (ROWS, 128))
    hidden = (xh * vector_of(vec_ref, "gain_one") + vector_of(vec_ref, "shift_one")).astype(BF)
    hid_ref[...] = hidden
    outs = []
    for g in range(4):
        cols = slice(GROUP * g, GROUP * (g + 1))
        _, w_inter = wb(g)
        at = PLACE["b_inter"][0] + FF_GROUP * g
        inter = dot(hidden[:, cols], w_inter) + vec_ref[:, at : at + FF_GROUP]
        inter_ref[:, FF_GROUP * g : FF_GROUP * (g + 1)] = inter
        act = (inter * gelu_parts(inter)).astype(BF)
        outs.append(dot(act, wc(g)))
    r2 = jnp.concatenate(outs, axis=1) + vector_of(vec_ref, "b_out") + hidden.astype(F32)
    xh, rs = norm_parts(r2)
    xh2_ref[...] = xh
    rs2_ref[...] = jnp.broadcast_to(rs, (ROWS, 128))
    y_ref[...] = (xh * vector_of(vec_ref, "gain_two") + vector_of(vec_ref, "shift_two")).astype(BF)


def norm_back(gy, xh, rs, gain):
    t = gy * gain
    m1 = jnp.mean(t, axis=-1, keepdims=True)
    m2 = jnp.mean(t * xh, axis=-1, keepdims=True)
    return rs[:, :1] * (t - m1 - xh * m2)


def layer_backward(gy, u_ref, wa, wb, wc, vec_ref, q_ref, k_ref, v_ref, p_ref, ctx_ref, xh1_ref, rs1_ref, hid_ref, inter_ref, xh2_ref, rs2_ref,
                   gu_ref, put_a, put_b, put_c, gvec_ref, gq_ref, gk_ref, gv_ref):
    def put_vec(name, row, start=0):
        at = PLACE[name][0] + start
        gvec_ref[:, at : at + row.shape[1]] = row

    def colsum(x):
        return jnp.sum(x.astype(F32), axis=0, keepdims=True)

    xh2 = xh2_ref[...]
    put_vec("gain_two", colsum(gy * xh2))
    put_vec("shift_two", colsum(gy))
    g_r2 = norm_back(gy, xh2, rs2_ref[...], vector_of(vec_ref, "gain_two"))
    g_out = g_r2.astype(BF)
    put_vec("b_out", colsum(g_out))
    hidden = hid_ref[...]
    hidden_t = hidden.T
    parts = []
    for g in range(4):
        cols = slice(GROUP * g, GROUP * (g + 1))
        wide = slice(FF_GROUP * g, FF_GROUP * (g + 1))
        inter = inter_ref[:, wide]
        half = gelu_parts(inter)
        act = (inter * half).astype(BF)
        slope = half + inter * (jnp.exp(-0.5 * inter * inter) * 0.3989422804014327)
        go = g_out[:, cols]
        put_c(g, dot(act.T, go))
        g_inter = (dot_nt(go, wc(g)) * slope).astype(BF)
        put_vec("b_inter", colsum(g_inter), FF_GROUP * g)
        put_b(g, dot(hidden_t[cols], g_inter))
        _, w_inter = wb(g)
        parts.append(dot_nt(g_inter, w_inter))
    g_hidden = (g_r2 + jnp.concatenate(parts, axis=1)).astype(BF).astype(F32)
    xh1 = xh1_ref[...]
    put_vec("gain_one", colsum(g_hidden * xh1))
    put_vec("shift_one", colsum(g_hidden))
    g_r1 = norm_back(g_hidden, xh1, rs1_ref[...], vector_of(vec_ref, "gain_one"))
    g_post = g_r1.astype(BF)
    put_vec("b_post", colsum(g_post))
    put_b(None, dot(ctx_ref[...].T, g_post))
    w_post, _ = wb(None)
    g_ctx = dot_nt(g_post, w_post).astype(BF)
    lane = lax.broadcasted_iota(jnp.int32, (ROWS, 128), 1)
    for pair in range(HEADS // 2):
        cols = slice(128 * pair, 128 * (pair + 1))
        qt, kt, vt, ct = q_ref[:, cols], k_ref[:, cols], v_ref[:, cols], g_ctx[:, cols]
        got = []
        for half in range(2):
            mine = (lane >= 64) if half else (lane < 64)
            cm = jnp.where(mine, ct, jnp.zeros_like(ct))
            p = p_ref[2 * pair + half]
            g_p = dot_nt(cm, vt)
            g_v = dot_tn(p.astype(BF), ct)
            g_s = (p * (g_p - jnp.sum(p * g_p, axis=-1, keepdims=True))).astype(BF)
            got.append((dot(g_s, kt) * 0.125, dot_tn(g_s, qt) * 0.125, g_v))
        gq_ref[:, cols] = jnp.where(lane < 64, got[0][0], got[1][0]).astype(BF)
        gk_ref[:, cols] = jnp.where(lane < 64, got[0][1], got[1][1]).astype(BF)
        gv_ref[:, cols] = jnp.where(lane < 64, got[0][2], got[1][2]).astype(BF)
    put_vec("b_qv", colsum(gq_ref[...]))
    put_vec("b_qv", colsum(gv_ref[...]), WIDTH)
    u_t = u_ref[...].T
    parts = []
    for g in range(4):
        cols = slice(GROUP * g, GROUP * (g + 1))
        gp = jnp.concatenate([gq_ref[:, cols], gk_ref[:, cols], gv_ref[:, cols]], axis=1)
        put_a(g, dot(u_t[cols], gp))
        parts.append(dot_nt(gp, wa(g)))
    gu_ref[...] = g_r1 + jnp.concatenate(parts, axis=1)


SIZE = 4
STRIDE = {"x": 16, "y": 4, "z": 1}
WORD_PART, WORD_STEP = 5120, 1280
ORDERS = (("z", "y", "x"), ("x", "z", "y"), ("y", "x", "z"))
VMEM = pl.BlockSpec(memory_space=pltpu.VMEM)
SMEM = pl.BlockSpec(memory_space=pltpu.SMEM)
HBM = pl.BlockSpec(memory_space=pl.ANY)
PARAMS = pltpu.CompilerParams(vmem_limit_bytes=56 << 20)


def spec_of(shape, dtype):
    return jax.ShapeDtypeStruct(shape, dtype)


def place_on(axis):
    return (lax.axis_index("dp") // STRIDE[axis]) % SIZE


def ring(block, axis, first_step, second_step):
    stride, route = STRIDE[axis], []
    for section, step in enumerate((first_step, second_step)):
        for chip in range(64):
            at = (chip // stride) % SIZE
            to = chip + ((at + step) % SIZE - at) * stride
            route.append((section * 64 + chip, section * 64 + to))
    return lax.ppermute(block, ("section", "dp"), route)


def cis(block, axis):
    return ring(block, axis, 1, -1)


def trans(block, axis):
    return ring(block, axis, -1, 1)


def swap(block):
    return lax.ppermute(block, "section", [(0, 1), (1, 0)])


def gather_stage(block, axis):
    near = cis(block, axis)
    other = trans(block, axis)
    return [block, near, other, cis(near, axis)]


def relative(axis):
    at = place_on(axis)
    sign = 1 - 2 * lax.axis_index("section")
    return [at, (at - sign) % SIZE, (at + sign) % SIZE, (at + 2) % SIZE]


def in_place(blocks, axis):
    which = relative(axis)
    ordered = []
    for spot in range(SIZE):
        picked = blocks[3]
        for number in range(3):
            picked = jnp.where(which[number] == spot, blocks[number], picked)
        ordered.append(picked)
    return ordered


def scatter_stage(blocks, axis):
    own, minus, plus, far = blocks
    first = cis(far, axis)
    third = trans(minus, axis)
    passed = (plus.astype(F32) + first.astype(F32)).astype(BF)
    second = cis(passed, axis)
    return own.astype(F32) + second.astype(F32) + third.astype(F32)


def stack_kernel(*refs):
    rows = refs[0].shape[0]
    for n in range(4):
        refs[4][n * rows : (n + 1) * rows] = refs[n][...]


def stack_rows(blocks):
    rows, columns = blocks[0].shape
    return pl.pallas_call(
        stack_kernel,
        grid=(columns // WORD_STEP,),
        out_shape=spec_of((4 * rows, columns), BF),
        in_specs=[pl.BlockSpec((rows, WORD_STEP), lambda i: (0, i))] * 4,
        out_specs=pl.BlockSpec((4 * rows, WORD_STEP), lambda i: (0, i)),
        name="stack_rows",
    )(*blocks)


def assemble_kernel(where_ref, *refs):
    ins, outs = refs[:12], refs[12:15]
    for n in range(4):
        outs[0][where_ref[0, n]] = ins[n][...]
        outs[1][:, where_ref[1, n]] = ins[4 + n][...]
        outs[2][:, where_ref[2, n]] = ins[8 + n][...]


A_SHAPE, B_SHAPE, C_SHAPE = (4, 192, 640), (4, 4, 48, 1536), (16, 4, 48, 192)


def assemble(blocks_a, blocks_b, blocks_c):
    where = jnp.stack([jnp.stack(relative(axis)) for axis in "xyz"]).astype(jnp.int32)
    return pl.pallas_call(
        assemble_kernel,
        out_shape=[spec_of(shape, BF) for shape in (A_SHAPE, B_SHAPE, C_SHAPE)],
        in_specs=[SMEM] + [VMEM] * 12,
        out_specs=[VMEM] * 3,
        compiler_params=PARAMS,
        name="assemble_weights",
    )(where, *blocks_a, *blocks_b, *blocks_c)


def fetch(layer, sec_ref, mine, other, held, sems):
    def bring(sources):
        copies = [pltpu.make_async_copy(sources[n], held[n], sems.at[n]) for n in range(3)]
        for copy in copies:
            copy.start()
        for copy in copies:
            copy.wait()

    @pl.when(sec_ref[0] == layer)
    def _():
        bring(mine)

    @pl.when(sec_ref[0] != layer)
    def _():
        bring(other)


def views(held):
    held_a, held_b, held_c = held

    def wa(g):
        return held_a[g][:, :576]

    def wb(g):
        if g is None:
            return held_b[...].reshape(WIDTH, 1536)[:, :WIDTH], None
        return None, held_b[g].reshape(GROUP, 1536)[:, WIDTH:]

    def wc(g):
        return held_c[4 * g : 4 * g + 4].reshape(FF_GROUP, GROUP)

    return wa, wb, wc


HELD = [pltpu.VMEM(shape, BF) for shape in (A_SHAPE, B_SHAPE, C_SHAPE)] + [pltpu.SemaphoreType.DMA((3,))]
KEPT = [
    spec_of((ROWS, WIDTH), BF),
    spec_of((ROWS, WIDTH), BF),
    spec_of((ROWS, WIDTH), BF),
    spec_of((HEADS, ROWS, ROWS), F32),
    spec_of((ROWS, WIDTH), BF),
    spec_of((ROWS, WIDTH), F32),
    spec_of((ROWS, 128), F32),
    spec_of((ROWS, WIDTH), BF),
    spec_of((ROWS, 4 * FF_GROUP), F32),
    spec_of((ROWS, WIDTH), F32),
    spec_of((ROWS, 128), F32),
]


def forward_kernel(layer, sec_ref, lengths_ref, u_ref, vec_ref, *refs):
    mine, other, outs, held, sems = refs[:3], refs[3:6], refs[6:18], refs[18:21], refs[21]
    fetch(layer, sec_ref, mine, other, held, sems)
    wa, wb, wc = views(held)
    source = jnp.where(sec_ref[0] == layer, 0, 1)
    layer_forward(u_ref, same_doc(lengths_ref, 2 * sec_ref[0]), wa, wb, wc, vec_ref.at[source], *outs)


def forward(layer, section, lengths, inputs, vectors, mine, other):
    outs = pl.pallas_call(
        functools.partial(forward_kernel, layer),
        out_shape=[spec_of((ROWS, WIDTH), BF)] + KEPT,
        in_specs=[SMEM, SMEM, VMEM, VMEM] + [HBM] * 6,
        out_specs=[VMEM] * 12,
        scratch_shapes=HELD,
        compiler_params=PARAMS,
        name="layer_forward",
    )(section, lengths, inputs, vectors, *mine, *other)
    return outs[0], outs[1:]


def backward_kernel(layer, sec_ref, gy_ref, u_ref, vec_ref, *refs):
    mine, other, kept = refs[:3], refs[3:6], refs[6:17]
    gu_ref, da_ref, db_ref, dc_ref = refs[17:21]
    held, sems, grads, gvec_ref, turned_ref = refs[21:24], refs[24], refs[25:28], refs[28], refs[29]
    fetch(layer, sec_ref, mine, other, held, sems)
    wa, wb, wc = views(held)

    def put_a(g, term):
        da_ref[g, :, :576] = term.astype(BF)

    def put_b(g, term):
        if g is None:
            db_ref[:, :, :, :WIDTH] = term.astype(BF).reshape(4, 4, 48, WIDTH)
        else:
            db_ref[g, :, :, WIDTH:] = term.astype(BF).reshape(4, 48, WIDTH)

    def put_c(g, term):
        dc_ref[4 * g : 4 * g + 4] = term.astype(BF).reshape(4, 4, 48, GROUP)

    source = jnp.where(sec_ref[0] == layer, 0, 1)
    gy = gy_ref[...].astype(BF).astype(F32) if layer == 0 else gy_ref[...]
    layer_backward(gy, u_ref, wa, wb, wc, vec_ref.at[source], *kept, gu_ref, put_a, put_b, put_c, gvec_ref, *grads)
    contract_into(gvec_ref, turned_ref, da_ref)


def backward(layer, section, gy, inputs, vectors, mine, other, kept):
    outs = pl.pallas_call(
        functools.partial(backward_kernel, layer),
        out_shape=[
            spec_of((ROWS, WIDTH), F32),
            spec_of(A_SHAPE, BF),
            spec_of(B_SHAPE, BF),
            spec_of(C_SHAPE, BF),
        ],
        in_specs=[SMEM, VMEM, VMEM, VMEM] + [HBM] * 6 + [VMEM] * 11,
        out_specs=[VMEM] * 4,
        scratch_shapes=HELD
        + [pltpu.VMEM((ROWS, WIDTH), BF)] * 3
        + [pltpu.VMEM((1, VECTOR), F32), pltpu.VMEM((128, WIDTH), F32)],
        compiler_params=PARAMS,
        name="layer_backward",
    )(section, gy, inputs, vectors, *mine, *other, *kept)
    return outs[0], outs[1:4]


def spreads():
    row = lax.broadcasted_iota(jnp.int32, (GROUP, 1), 0)
    device = row // 12
    within = row - 12 * device
    wide = [48 * device + within + 12 * n for n in range(4)]
    lane = lax.broadcasted_iota(jnp.int32, (GROUP, FF_GROUP), 1)
    inter = [(lane == target).astype(F32).astype(BF) for target in wide]
    row = lax.broadcasted_iota(jnp.int32, (96, 1), 0)
    device = row // 12
    within = row - 12 * device
    lane = lax.broadcasted_iota(jnp.int32, (96, GROUP), 1)
    heads = [(lane == 24 * device + within + 12 * n).astype(F32).astype(BF) for n in range(2)]
    return inter, heads


def expand_kernel(mine_ref, other_ref, out_ref):
    inter, heads = spreads()
    for source, ref in enumerate((mine_ref, other_ref)):
        turned = ref[...].reshape(WIDTH, 640)[:, 512:].astype(F32).T
        for name, (offset, width) in SHARD.items():
            at = PLACE[name][0]
            lane = 64 + offset // 12
            if name == "b_inter":
                for g in range(4):
                    rows = turned[lane : lane + 4, GROUP * g : GROUP * (g + 1)].astype(BF)
                    value = sum(dot(rows, inter[n])[n : n + 1] for n in range(4))
                    out_ref[source, :, at + FF_GROUP * g : at + FF_GROUP * (g + 1)] = value
            elif name == "b_qv":
                for e in range(8):
                    rows = turned[lane : lane + 2, 96 * e : 96 * (e + 1)].astype(BF)
                    value = sum(dot(rows, heads[n])[n : n + 1] for n in range(2))
                    out_ref[source, :, at + GROUP * e : at + GROUP * (e + 1)] = value
            else:
                out_ref[source, :, at : at + WIDTH] = turned[lane : lane + 1]


def expand(mine, other):
    return pl.pallas_call(
        expand_kernel,
        out_shape=spec_of((2, 1, VECTOR), F32),
        in_specs=[VMEM] * 2,
        out_specs=VMEM,
        compiler_params=PARAMS,
        name="expand_vectors",
    )(mine, other)


def contract_into(gvec_ref, turned_ref, da_ref):
    inter, heads = spreads()
    turned_ref[...] = jnp.zeros_like(turned_ref)
    for name, (offset, width) in SHARD.items():
        at = PLACE[name][0]
        lane = 64 + offset // 12
        if name == "b_inter":
            for g in range(4):
                value = gvec_ref[:, at + FF_GROUP * g : at + FF_GROUP * (g + 1)].astype(BF)
                for n in range(4):
                    turned_ref[lane + n : lane + n + 1, GROUP * g : GROUP * (g + 1)] = dot_nt(value, inter[n])
        elif name == "b_qv":
            for e in range(8):
                value = gvec_ref[:, at + GROUP * e : at + GROUP * (e + 1)].astype(BF)
                for n in range(2):
                    turned_ref[lane + n : lane + n + 1, 96 * e : 96 * (e + 1)] = dot_nt(value, heads[n])
        else:
            turned_ref[lane : lane + 1] = gvec_ref[:, at : at + WIDTH]
    columns = turned_ref[...].T.astype(BF)
    for g in range(4):
        da_ref[g, :, 576:] = columns[GROUP * g : GROUP * (g + 1), 64:]


def table_kernel(lhs_ref, grad_ref, *outs):
    for n in range(4):
        outs[n][...] = dot_nt(lhs_ref[GROUP * n : GROUP * (n + 1)], grad_ref[...]).astype(BF)


def table_terms(part, turned, logit_grad):
    steps = WORD_PART // WORD_STEP
    return pl.pallas_call(
        table_kernel,
        grid=(steps,),
        out_shape=[spec_of((GROUP, WORD_PART), BF)] * 4,
        in_specs=[
            pl.BlockSpec((WIDTH, 256), lambda i: (part, 0)),
            pl.BlockSpec((WORD_STEP, 256), lambda i: (steps * part + i, 0)),
        ],
        out_specs=[pl.BlockSpec((GROUP, WORD_STEP), lambda i: (0, i))] * 4,
        compiler_params=PARAMS,
        name="table_terms",
    )(turned, logit_grad)


def head_grad_kernel(part, words, grad_ref, *refs):
    ins, out_ref = refs[:4], refs[4]
    step = pl.program_id(0)
    grad = grad_ref[...]
    if (part + 1) * WORD_PART > words:
        column = lax.broadcasted_iota(jnp.int32, grad.shape, 0) + (part * WORD_PART + step * WORD_STEP)
        grad = jnp.where(column < words, grad, jnp.zeros_like(grad))

    @pl.when(step == 0)
    def _():
        out_ref[...] = jnp.zeros_like(out_ref)

    table = jnp.concatenate([block[...] for block in ins], axis=0)
    out_ref[...] += dot(table, grad)


def head_grad(part, logit_grad, blocks):
    steps = WORD_PART // WORD_STEP
    return pl.pallas_call(
        functools.partial(head_grad_kernel, part, logit_grad.shape[0]),
        grid=(steps,),
        out_shape=spec_of((WIDTH, 256), F32),
        in_specs=[pl.BlockSpec((WORD_STEP, 256), lambda i: (steps * part + i, 0))]
        + [pl.BlockSpec((GROUP, WORD_STEP), lambda i: (0, i))] * 4,
        out_specs=pl.BlockSpec((WIDTH, 256), lambda i: (0, 0)),
        compiler_params=PARAMS,
        name="head_grad",
    )(logit_grad, *blocks)


def unpermute_kernel(a_ref, b_ref, c_ref, pick_ref, out_ref):
    total = jnp.zeros((256, WIDTH), F32)
    for part, ref in enumerate((a_ref, b_ref, c_ref)):
        value = ref[...]
        high = value.astype(BF)
        rest = (value - high.astype(F32)).astype(BF)
        pick = pick_ref[WIDTH * part : WIDTH * (part + 1)]
        total = total + dot_tn(high, pick) + dot_tn(rest, pick)
    out_ref[...] = total


def unpermute(terms, pick):
    return pl.pallas_call(
        unpermute_kernel,
        out_shape=spec_of((256, WIDTH), F32),
        in_specs=[VMEM] * 4,
        out_specs=VMEM,
        compiler_params=PARAMS,
        name="unpermute",
    )(*terms, pick)


def logits_kernel(lhs_ref, *refs):
    ins, out_ref = refs[:4], refs[-1]
    table = jnp.concatenate([block[...] for block in ins], axis=0)
    out_ref[...] = dot(lhs_ref[...], table).astype(BF).T


def logits_part(part, straight, blocks, words, before):
    steps = WORD_PART // WORD_STEP
    extra = [] if before is None else [before]
    return pl.pallas_call(
        logits_kernel,
        grid=(steps,),
        out_shape=spec_of((words, 256), BF),
        in_specs=[pl.BlockSpec((256, WIDTH), lambda i: (0, part))]
        + [pl.BlockSpec((GROUP, WORD_STEP), lambda i: (0, i))] * 4
        + [HBM] * len(extra),
        out_specs=pl.BlockSpec((WORD_STEP, 256), lambda i: (steps * part + i, 0)),
        input_output_aliases={5: 0} if extra else {},
        compiler_params=PARAMS,
        name="logits",
    )(straight, *blocks, *extra)


def combine_kernel(sec_ref, where_ref, *refs):
    kept, came, outs = refs[:6], refs[6:12], refs[12:24]
    bufs, sems = refs[24:30], refs[30]

    def bring(layer):
        copies = []
        for n in range(3):
            copies.append(pltpu.make_async_copy(kept[3 * layer + n], bufs[n], sems.at[n]))
            copies.append(pltpu.make_async_copy(came[3 * layer + n], bufs[3 + n], sems.at[3 + n]))
        for copy in copies:
            copy.start()
        for copy in copies:
            copy.wait()

    @pl.when(sec_ref[0] == 0)
    def _():
        bring(0)

    @pl.when(sec_ref[0] != 0)
    def _():
        bring(1)

    def added(first, second):
        return (first.astype(F32) + second.astype(F32)).astype(BF)

    for n in range(4):
        a, b, c = where_ref[0, n], where_ref[1, n], where_ref[2, n]
        outs[n][...] = added(bufs[0][a], bufs[3][a])
        outs[4 + n][...] = added(bufs[1][:, b], bufs[4][:, b])
        outs[8 + n][...] = added(bufs[2][:, c], bufs[5][:, c])


def combine(section, kept, came):
    where = jnp.stack([jnp.stack(relative(axis)) for axis in "xyz"]).astype(jnp.int32)
    shapes = [(192, 640)] * 4 + [(4, 48, 1536)] * 4 + [(16, 48, 192)] * 4
    outs = pl.pallas_call(
        combine_kernel,
        out_shape=[spec_of(shape, BF) for shape in shapes],
        in_specs=[SMEM, SMEM] + [HBM] * 12,
        out_specs=[VMEM] * 12,
        scratch_shapes=[pltpu.VMEM(shape, BF) for shape in (A_SHAPE, B_SHAPE, C_SHAPE) * 2]
        + [pltpu.SemaphoreType.DMA((6,))],
        compiler_params=PARAMS,
        name="combine_grads",
    )(section, where, *kept, *came)
    return outs[:4], outs[4:8], outs[8:]


def feature_picks():
    picks = []
    for order in ORDERS:
        steps = [jnp.stack(relative(axis)) * (12 * STRIDE[axis]) for axis in order[::-1]]
        feature = (
            steps[0][:, None, None, None]
            + steps[1][None, :, None, None]
            + steps[2][None, None, :, None]
            + jnp.arange(12)[None, None, None, :]
        ).reshape(WIDTH)
        picks.append(feature)
    feature = jnp.concatenate(picks)
    return (feature[:, None] == jnp.arange(WIDTH)[None, :]).astype(BF)


def per_device(
    tokens, lengths, w_qkv, b_qv, w_post, b_post, gain_one, shift_one, w_inter, b_inter, w_out, b_out, gain_two, shift_two,
    embed_table, logit_grad,
):
    section_index = lax.axis_index("section")
    section = section_index.astype(jnp.int32)[None]
    is_first = section_index == 0
    words = embed_table.shape[1]
    given = dict(b_qv=b_qv, b_inter=b_inter, b_post=b_post, gain_one=gain_one, shift_one=shift_one, b_out=b_out, gain_two=gain_two, shift_two=shift_two)
    shard = jnp.concatenate([given[name][0].astype(BF) for name in SHARD]).reshape(12, 12).T

    both = jnp.concatenate([w_qkv[0].astype(BF), shard, jnp.zeros((12, 52), BF), w_post[0].astype(BF), w_inter[0].astype(BF)], axis=1)
    both = jnp.concatenate(in_place(gather_stage(both, "z"), "z"), axis=0)
    part_a = jnp.concatenate(in_place(gather_stage(both[:, :640], "y"), "y"), axis=0)
    part_b = jnp.stack(in_place(gather_stage(both[:, 640:], "x"), "x"), axis=0)
    part_c = jnp.stack(in_place(gather_stage(w_out[0].astype(BF), "y"), "y"), axis=0)
    part_c = jnp.concatenate(in_place(gather_stage(part_c, "x"), "x"), axis=0)
    mine = assemble(gather_stage(part_a, "x"), gather_stage(part_b, "y"), gather_stage(part_c, "z"))
    other = [swap(piece) for piece in mine]
    vectors = expand(mine[0], other[0])

    table_low = jnp.pad(embed_table.astype(BF), ((0, 0), (0, 3 * WORD_PART - words)))
    table = []
    for part, order in enumerate(ORDERS):
        rows = table_low[:, WORD_PART * part : WORD_PART * (part + 1)]
        rows = jnp.concatenate(gather_stage(rows, order[0]), axis=0)
        rows = stack_rows(gather_stage(rows, order[1]))
        table.append(gather_stage(rows, order[2]))

    inputs = lax.dynamic_slice_in_dim(tokens, section_index * ROWS, ROWS, 0)
    middle, kept_zero = forward(0, section, lengths, inputs, vectors, mine, other)
    top, kept_one = forward(1, section, lengths, middle, vectors, mine, other)

    pick = feature_picks()
    grad_turned = logit_grad.T
    top_other = swap(top)
    top_rows = jnp.concatenate([jnp.where(is_first, top, top_other), jnp.where(is_first, top_other, top)], axis=0)
    turned = dot_nt(pick, top_rows).astype(BF)
    straight = dot_nt(top_rows, pick).astype(BF)
    table_sums = []
    for part, order in enumerate(ORDERS):
        total = scatter_stage(table_terms(part, turned, grad_turned), order[2]).astype(BF)
        total = scatter_stage([total[48 * n : 48 * (n + 1)] for n in range(4)], order[1]).astype(BF)
        total = scatter_stage([total[12 * n : 12 * (n + 1)] for n in range(4)], order[0])
        table_sums.append(total)
    table_grad = jnp.concatenate(table_sums, axis=1)[:, :words]

    grad_rows = unpermute([head_grad(part, grad_turned, table[part]) for part in range(3)], pick)
    came = swap(lax.dynamic_slice_in_dim(grad_rows, (1 - section_index) * ROWS, ROWS, 0))
    grad_top = lax.dynamic_slice_in_dim(grad_rows, section_index * ROWS, ROWS, 0) + came
    grad_middle, terms_one = backward(1, section, grad_top, middle, vectors, mine, other, kept_one)
    came_one = [lax.ppermute(term, "section", [(0, 1)]) for term in terms_one]
    grad_inputs, terms_zero = backward(0, section, grad_middle, inputs, vectors, mine, other, kept_zero)
    came_zero = [lax.ppermute(term, "section", [(1, 0)]) for term in terms_zero]

    token_low = grad_inputs.astype(BF)
    half = WIDTH // 2
    own_half = lax.dynamic_slice_in_dim(token_low, section_index * half, half, 1)
    came_half = swap(lax.dynamic_slice_in_dim(token_low, (1 - section_index) * half, half, 1))
    token_out = jnp.concatenate([jnp.where(is_first, own_half, came_half), jnp.where(is_first, came_half, own_half)], axis=0)

    parts_a, parts_b, parts_c = combine(section, [*terms_zero, *terms_one], [*came_zero, *came_one])

    def picked(pieces, axis):
        return [lax.dynamic_index_in_dim(pieces, at, 0, keepdims=False) for at in relative(axis)]

    sum_a = scatter_stage(parts_a, "x").astype(BF)
    sum_b = scatter_stage(parts_b, "y").astype(BF)
    sum_c = scatter_stage(parts_c, "z").astype(BF)
    sum_a = scatter_stage(picked(sum_a.reshape(4, 48, 640), "y"), "y").astype(BF)
    sum_b = scatter_stage(picked(sum_b, "x"), "x").astype(BF)
    sum_c = scatter_stage(picked(sum_c.reshape(4, 4, 48, 192), "x"), "x").astype(BF)
    sum_c = scatter_stage(picked(sum_c, "y"), "y")
    sum_ab = jnp.concatenate([sum_a, sum_b], axis=1).reshape(4, 12, 640 + 1536)
    sum_ab = scatter_stage(picked(sum_ab, "z"), "z")

    sums = {"w_qkv": sum_ab[:, :576], "w_post": sum_ab[:, 640 : 640 + WIDTH], "w_inter": sum_ab[:, 640 + WIDTH :], "w_out": sum_c}
    vec_sums = sum_ab[:, 576:588].T
    for name, (offset, width) in SHARD.items():
        sums[name] = vec_sums[offset // 12 : (offset + width) // 12].reshape(width)
    names = ("w_qkv", "b_qv", "w_post", "b_post", "gain_one", "shift_one", "w_inter", "b_inter", "w_out", "b_out", "gain_two", "shift_two")
    logits = None
    for part in range(3):
        logits = logits_part(part, straight, table[part], words, logits)
    return (logits.T, token_out) + tuple(sums[name][None] for name in names) + (table_grad,)


def solution(mesh):
    matrix, vector = P("section", "dp", None), P("section", "dp")
    weights = (matrix, vector, matrix, vector, vector, vector, matrix, vector, matrix, vector, vector, vector)
    return jax.shard_map(
        per_device,
        mesh=mesh,
        in_specs=(P("dp", None), P("dp", None)) + weights + (P("dp", "section"), P("dp", "section")),
        out_specs=(P("dp", "section"), P("dp", "section")) + weights + (P("dp", "section"),),
        check_vma=False,
    )
```

time: 1830 us -> 523 us (0.29)
  blocking collectives: 1110 us -> 0 us
  local copies, waits for them, and re-layouts: 240 us -> 16 us
  matrix products: 193 us -> 5.38 us
  waiting for transfers between devices: 19.6 us -> 187 us
  Pallas kernels: 0 us -> 146 us
  other arithmetic: 87.6 us -> 35.4 us
  between operations: 23.2 us -> 2.69 us
  starting transfers between devices: 139 us -> 120 us
    unnamed x3 -> x0, blocking collectives: 928 us -> none
    dot_general x93 -> x2, matrix products: 193 us -> 5.38 us  [dot_nt(): lax.dot_general(a, b, (((1,), (1,)), ((), ())), preferred_element_type=F32)]
    ppermute x10 -> x114, waiting for transfers between devices: 4.4 us -> 187 us  [the longest x102 185 us: ring(): return lax.ppermute(block, ('section', 'dp'), route)]
    all_gather x1 -> x0, blocking collectives: 180 us -> none  [per_device(): lax.all_gather(shards[0], 'dp', axis=0, tiled=True)]
    pallas_call x0 -> x20, Pallas kernels: none -> 146 us  [the longest x2 30.7 us: backward(): pl.pallas_call(functools.partial(backward_kernel, layer), out_shape=[spec...]
    unnamed x50 -> x0, starting transfers between devices: 122 us -> none
    ppermute x10 -> x114, starting transfers between devices: 17 us -> 120 us  [the longest x102 101 us: ring(): return lax.ppermute(block, ('section', 'dp'), route)]
    unnamed x584 -> x116, local copies, waits for them, and re-layouts: 90.3 us -> 10.5 us
  transfers between devices with their start and end apart: 65 -> 114, of which waited for: 5 -> 45; matrix products, arithmetic and copies ran while one was open for 27% -> 9% of each run, Pallas kernels for 0% -> 29%
where the time goes in v1:
time: 523 us; the launch traced here: 513 us
  waiting for transfers between devices  187 us (36%)
  Pallas kernels  146 us (28%)
  starting transfers between devices  120 us (23%)
  other arithmetic  35.4 us (7%)
  local copies, waits for them, and re-layouts  16 us (3%)
  matrix products  5.38 us (1%)
    ppermute x102, waiting for transfers between devices, ring(): return lax.ppermute(block, ('section', 'dp'), route)  185 us
    ppermute x102, starting transfers between devices, ring(): return lax.ppermute(block, ('section', 'dp'), route)  101 us
    pallas_call x2, Pallas kernels, backward(): pl.pallas_call(functools.partial(backward_kernel, layer), out_shape=[spec...  30.7 us
    pallas_call x2, Pallas kernels, forward(): pl.pallas_call(functools.partial(forward_kernel, layer), out_shape=[spec_...  20.8 us
    pallas_call x3, Pallas kernels, logits_part(): pl.pallas_call(logits_kernel, grid=(steps,), out_shape=spec_of((words, 25...  20.7 us
    pallas_call x3, Pallas kernels, head_grad(): pl.pallas_call(functools.partial(head_grad_kernel, part, logit_grad.shape...  20.4 us
    pallas_call x3, Pallas kernels, table_terms(): pl.pallas_call(table_kernel, grid=(steps,), out_shape=[spec_of((GROUP, WO...  19.7 us
    pallas_call x3, Pallas kernels, stack_rows(): pl.pallas_call(stack_kernel, grid=(columns // WORD_STEP,), out_shape=spec...  11.6 us
  transfers between devices with their start and end apart: 114, of which 45 were waited for; matrix products, arithmetic and copies ran while one was open for 9% of the time, Pallas kernels for 29%

profile of v1, /device:TPU:0, one launch (start us, length us, event | category | flops | bytes accessed | tf_op | source)
XLA Modules:
  0.0 513.1 jit_solution(11659824971309056113)
XLA Ops:
  18.4 4.4 collective-permute-done.17
  66.3 4.2 collective-permute-done.6.refs_1_
  72.9 5.8 %collective-permute-done.8.refs_3_ = bf16[192,640]{1,0:T(8,128)(2,1)S(1)} collective-permute-done((bf16[192,640]{1,0:T(8,128)(2,1)S(1)}, bf16[192,640]{1,0:T(8,128)(2,1)S(1)}, u32[]{:S(2)}, u32[]{:S(2)}) %collective-permute-start.8) | collective-permute-done | bytes 245792 | tf_op jit(solution)/shard_map/ppermute | solution.py:217
  81.4 4.4 collective-permute-start.50
  90.8 5.0 assemble_weights.1
  113.2 4.5 collective-permute-done.42.refs_3_
  124.5 19.6 %collective-permute-done.52.refs_1_ = bf16[192,5120]{1,0:T(8,128)(2,1)} collective-permute-done((bf16[192,5120]{1,0:T(8,128)(2,1)}, bf16[192,5120]{1,0:T(8,128)(2,1)}, u32[]{:S(2)}, u32[]{:S(2)}) %collective-permute-start.52) | collective-permute-done | bytes 1966112 | tf_op jit(solution)/shard_map/ppermute | solution.py:217
  149.3 10.3 %layer_forward.2 = (bf16[128,768]{1,0:T(8,128)(2,1)}, bf16[128,768]{1,0:T(8,128)(2,1)}, bf16[128,768]{1,0:T(8,128)(2,1)}, bf16[128,768]{1,0:T(8,128)(2,1)}, f32[...) custom-call(s32[1]{0:T(128)} %bitcast.sec_ref, ...), custom_call_target="tpu_custom_call" | custom-call | tf_op jit(solution)/shard_map/layer_forward/pallas_call | solution.py:364
  159.6 10.5 %layer_forward.3 = (bf16[128,768]{1,0:T(8,128)(2,1)}, bf16[128,768]{1,0:T(8,128)(2,1)}, bf16[128,768]{1,0:T(8,128)(2,1)}, bf16[128,768]{1,0:T(8,128)(2,1)}, f32[...) custom-call(s32[1]{0:T(128)} %bitcast.sec_ref, ...), custom_call_target="tpu_custom_call" | custom-call | tf_op jit(solution)/shard_map/layer_forward/pallas_call | solution.py:364
  178.4 6.6 %table_terms.5 = (bf16[192,5120]{1,0:T(8,128)(2,1)}, bf16[192,5120]{1,0:T(8,128)(2,1)}, bf16[192,5120]{1,0:T(8,128)(2,1)}, bf16[192,5120]{1,0:T(8,128)(2,1)}) custom-call(bf16[2304,256]{1,0:T(8,128)(2,1)} %fusion.4.lhs_ref, bf16[15264,256]{1,0:T(8,128)(2,1)} %bitcast.125), custom_call_target="tpu_custom_call" | custom-call | tf_op jit(solution)/shard_map/table_terms/pallas_call | solution.py:498
  187.8 6.7 %head_grad.3.a_ref = f32[768,256]{1,0:T(8,128)} custom-call(bf16[15264,256]{1,0:T(8,128)(2,1)} %bitcast.126, bf16[192,5120]{1,0:T(8,128)(2,1)} %stack_rows.5.refs_0_, bf16[192,5120]{1,0:T(8,128)(2,1)} %collective-permute-done.52.refs_1_, bf16[192,5120]{1,0:T(8,128)(2,1)} %collective-permute-done.53.refs_2_, bf16[192,5120]{1,0:T(8,128)(2,1)} %collective-permute-done.54.refs_3_), custom_call_target="tpu_custom_call" | custom-call | tf_op jit(solution)/shard_map/head_grad/pallas_call | solution.py:530
  194.5 21.5 %collective-permute-done.44.refs_2_ = bf16[192,5120]{1,0:T(8,128)(2,1)} collective-permute-done((bf16[192,5120]{1,0:T(8,128)(2,1)}, bf16[192,5120]{1,0:T(8,128)(2,1)}, u32[]{:S(2)}, u32[]{:S(2)}) %collective-permute-start.44) | collective-permute-done | bytes 1966112 | tf_op jit(solution)/shard_map/ppermute | solution.py:217
  217.1 6.7 %head_grad.4.b_ref = f32[768,256]{1,0:T(8,128)} custom-call(bf16[15264,256]{1,0:T(8,128)(2,1)} %bitcast.127, bf16[192,5120]{1,0:T(8,128)(2,1)} %stack_rows.4.refs_0_, bf16[192,5120]{1,0:T(8,128)(2,1)} %collective-permute-done.43.refs_1_, bf16[192,5120]{1,0:T(8,128)(2,1)} %collective-permute-done.44.refs_2_, bf16[192,5120]{1,0:T(8,128)(2,1)} %collective-permute-done.45.refs_3_), custom_call_target="tpu_custom_call" | custom-call | tf_op jit(solution)/shard_map/head_grad/pallas_call | solution.py:530
  223.8 6.9 %head_grad.5.c_ref = f32[768,256]{1,0:T(8,128)} custom-call(bf16[15264,256]{1,0:T(8,128)(2,1)} %bitcast.128, bf16[192,5120]{1,0:T(8,128)(2,1)} %stack_rows.3.refs_0_, bf16[192,5120]{1,0:T(8,128)(2,1)} %collective-permute-done.34.refs_1_, bf16[192,5120]{1,0:T(8,128)(2,1)} %collective-permute-done.35.refs_2_, bf16[192,5120]{1,0:T(8,128)(2,1)} %collective-permute-done.36.refs_3_), custom_call_target="tpu_custom_call" | custom-call | tf_op jit(solution)/shard_map/head_grad/pallas_call | solution.py:530
  230.7 5.7 %unpermute.1 = f32[256,768]{1,0:T(8,128)} custom-call(f32[768,256]{1,0:T(8,128)} %head_grad.3.a_ref, f32[768,256]{1,0:T(8,128)} %head_grad.4.b_ref, f32[768,256]{1,0:T(8,128)} %head_grad.5.c_ref, bf16[2304,768]{1,0:T(8,128)(2,1)} %fusion.1.pick_ref), custom_call_target="tpu_custom_call" | custom-call | tf_op jit(solution)/shard_map/unpermute/pallas_call | solution.py:554
  237.6 6.5 %table_terms.4 = (bf16[192,5120]{1,0:T(8,128)(2,1)}, bf16[192,5120]{1,0:T(8,128)(2,1)}, bf16[192,5120]{1,0:T(8,128)(2,1)}, bf16[192,5120]{1,0:T(8,128)(2,1)}) custom-call(bf16[2304,256]{1,0:T(8,128)(2,1)} %fusion.4.lhs_ref, bf16[15264,256]{1,0:T(8,128)(2,1)} %bitcast.129), custom_call_target="tpu_custom_call" | custom-call | tf_op jit(solution)/shard_map/table_terms/pallas_call | solution.py:498
  244.1 6.6 %table_terms.3 = (bf16[192,5120]{1,0:T(8,128)(2,1)}, bf16[192,5120]{1,0:T(8,128)(2,1)}, bf16[192,5120]{1,0:T(8,128)(2,1)}, bf16[192,5120]{1,0:T(8,128)(2,1)}) custom-call(bf16[2304,256]{1,0:T(8,128)(2,1)} %fusion.4.lhs_ref, bf16[15264,256]{1,0:T(8,128)(2,1)} %bitcast.130), custom_call_target="tpu_custom_call" | custom-call | tf_op jit(solution)/shard_map/table_terms/pallas_call | solution.py:498
  252.0 15.2 %layer_backward.2 = (f32[128,768]{1,0:T(8,128)}, bf16[4,192,640]{2,1,0:T(8,128)(2,1)}, bf16[4,4,48,1536]{3,2,1,0:T(8,128)(2,1)}, bf16[16,4,48,192]{3,2,1,0:T(8,128)(2,1)}) custom-call(s32[1]{0:T(128)} %bitcast.sec_ref, f32[128,768]{1,0:T(8,128)} %dynamic-slice_add_fusion.gy_ref, bf16[128,768]{1,0:T(8,128)(2,1)} %get-tuple-element.77.u_ref, ...), custom_call_target="tpu_custom_call" | custom-call | tf_op jit(solution)/shard_map/layer_backward/pallas_call | solution.py:402
  267.2 15.5 %layer_backward.3 = (f32[128,768]{1,0:T(8,128)}, bf16[4,192,640]{2,1,0:T(8,128)(2,1)}, bf16[4,4,48,1536]{3,2,1,0:T(8,128)(2,1)}, bf16[16,4,48,192]{3,2,1,0:T(8,128)(2,1)}) custom-call(s32[1]{0:T(128)} %bitcast.sec_ref, f32[128,768]{1,0:T(8,128)} %get-tuple-element.90.gy_ref, bf16[128,768]{1,0:T(8,128)(2,1)} %constant_dynamic-slice_fusion.2.u_ref, ...), custom_call_target="tpu_custom_call" | custom-call | tf_op jit(solution)/shard_map/layer_backward/pallas_call | solution.py:402
  289.9 6.8 %logits.3.refs_4_ = bf16[15264,256]{1,0:T(8,128)(2,1)} custom-call(bf16[256,2304]{1,0:T(8,128)(2,1)} %fusion.3.lhs_ref, bf16[192,5120]{1,0:T(8,128)(2,1)} %stack_rows.5.refs_0_, bf16[192,5120]{1,0:T(8,128)(2,1)} %collective-permute-done.52.refs_1_, bf16[192,5120]{1,0:T(8,128)(2,1)} %collective-permute-done.53.refs_2_, ...), custom_call_target="tpu_custom_call" | custom-call | tf_op jit(solution)/shard_map/logits/pallas_call | solution.py:573
  296.7 6.8 %logits.4.refs_4_ = bf16[15264,256]{1,0:T(8,128)(2,1)} custom-call(bf16[256,2304]{1,0:T(8,128)(2,1)} %fusion.3.lhs_ref, bf16[192,5120]{1,0:T(8,128)(2,1)} %stack_rows.4.refs_0_, bf16[192,5120]{1,0:T(8,128)(2,1)} %collective-permute-done.43.refs_1_, bf16[192,5120]{1,0:T(8,128)(2,1)} %collective-permute-done.44.refs_2_, ...), custom_call_target="tpu_custom_call", output_to_operand_aliasing={{}: (5, {})} | custom-call | tf_op jit(solution)/shard_map/logits/pallas_call | solution.py:573
  303.5 7.1 %logits.5 = bf16[15264,256]{1,0:T(8,128)(2,1)} custom-call(bf16[256,2304]{1,0:T(8,128)(2,1)} %fusion.3.lhs_ref, bf16[192,5120]{1,0:T(8,128)(2,1)} %stack_rows.3.refs_0_, bf16[192,5120]{1,0:T(8,128)(2,1)} %collective-permute-done.34.refs_1_, bf16[192,5120]{1,0:T(8,128)(2,1)} %collective-permute-done.35.refs_2_, ...), custom_call_target="tpu_custom_call", output_to_operand_aliasing={{}: (5, {})} | custom-call | tf_op jit(solution)/shard_map/logits/pallas_call | solution.py:573
  341.4 7.7 %combine_grads.1 = (bf16[192,640]{1,0:T(8,128)(2,1)}, bf16[192,640]{1,0:T(8,128)(2,1)}, bf16[192,640]{1,0:T(8,128)(2,1)}, bf16[192,640]{1,0:T(8,128)(2,1)}, bf16...) custom-call(s32[1]{0:T(128)} %bitcast.sec_ref, ...), custom_call_target="tpu_custom_call" | custom-call | tf_op jit(solution)/shard_map/combine_grads/pallas_call | solution.py:622
  356.3 24.0 %collective-permute-done.98 = bf16[192,5120]{1,0:T(8,128)(2,1)} collective-permute-done((bf16[192,5120]{1,0:T(8,128)(2,1)}, bf16[192,5120]{1,0:T(8,128)(2,1)}, u32[]{:S(2)}, u32[]{:S(2)}) %collective-permute-start.98) | collective-permute-done | bytes 1966112 | tf_op jit(solution)/shard_map/ppermute | solution.py:217
  397.1 7.2 %collective-permute-done.64 = bf16[192,640]{1,0:T(8,128)(2,1)S(1)} collective-permute-done((bf16[192,640]{1,0:T(8,128)(2,1)S(1)}, bf16[192,640]{1,0:T(8,128)(2,1)S(1)}, u32[]{:S(2)}, u32[]{:S(2)}) %collective-permute-start.64) | collective-permute-done | bytes 245792 | tf_op jit(solution)/shard_map/ppermute | solution.py:217
  404.6 5.3 %collective-permute-done.66 = bf16[48,640]{1,0:T(8,128)(2,1)S(1)} collective-permute-done((bf16[48,640]{1,0:T(8,128)(2,1)S(1)}, bf16[48,640]{1,0:T(8,128)(2,1)S(1)}, u32[]{:S(2)}, u32[]{:S(2)}) %collective-permute-start.66) | collective-permute-done | bytes 61472 | tf_op jit(solution)/shard_map/ppermute | solution.py:217
  419.0 5.8 %collective-permute-done.81 = bf16[4,48,192]{2,1,0:T(8,128)(2,1)S(1)} collective-permute-done((bf16[4,48,192]{2,1,0:T(8,128)(2,1)S(1)}, bf16[4,48,192]{2,1,0:T(8,128)(2,1)S(1)}, u32[]{:S(2)}, u32[]{:S(2)}) %collective-permute-start.81) | collective-permute-done | bytes 73760 | tf_op jit(solution)/shard_map/ppermute | solution.py:217
  432.6 8.2 %collective-permute-done.84 = bf16[48,192]{1,0:T(8,128)(2,1)S(1)} collective-permute-done((bf16[48,192]{1,0:T(8,128)(2,1)S(1)}, bf16[48,192]{1,0:T(8,128)(2,1)S(1)}, u32[]{:S(2)}, u32[]{:S(2)}) %collective-permute-start.84) | collective-permute-done | bytes 18464 | tf_op jit(solution)/shard_map/ppermute | solution.py:217
  453.8 5.6 %collective-permute-done.100 = bf16[48,5120]{1,0:T(8,128)(2,1)S(1)} collective-permute-done((bf16[48,5120]{1,0:T(8,128)(2,1)S(1)}, bf16[48,5120]{1,0:T(8,128)(2,1)S(1)}, u32[]{:S(2)}, u32[]{:S(2)}) %collective-permute-start.100) | collective-permute-done | bytes 491552 | tf_op jit(solution)/shard_map/ppermute | solution.py:217
  481.3 6.4 %collective-permute-done.112 = bf16[12,5120]{1,0:T(8,128)(2,1)S(1)} collective-permute-done((bf16[12,5120]{1,0:T(8,128)(2,1)S(1)}, bf16[12,5120]{1,0:T(8,128)(2,1)S(1)}, u32[]{:S(2)}, u32[]{:S(2)}) %collective-permute-start.112) | collective-permute-done | bytes 122912 | tf_op jit(solution)/shard_map/ppermute | solution.py:217
  487.9 6.3 %collective-permute-done.73 = bf16[48,1536]{1,0:T(8,128)(2,1)S(1)} collective-permute-done((bf16[48,1536]{1,0:T(8,128)(2,1)S(1)}, bf16[48,1536]{1,0:T(8,128)(2,1)S(1)}, u32[]{:S(2)}, u32[]{:S(2)}) %collective-permute-start.73) | collective-permute-done | bytes 147488 | tf_op jit(solution)/shard_map/ppermute | solution.py:217
  501.0 4.5 collective-permute-done.76
  (443 shorter events, 242.1 us)
Async XLA Ops:
  15.6 33.6 %collective-permute-start.47 = (bf16[12,5120]{1,0:T(8,128)(2,1)S(1)}, bf16[12,5120]{1,0:T(8,128)(2,1)S(1)}, u32[]{:S(2)}, u32[]{:S(2)}) collective-permute-start(bf16[12,5120]{1,0:T(8,128)(2,1)S(1)} %get-tuple-element.172), channel_id=1, source_target_pairs={{0,3},{1,0},{2,1},{3,2},{4,7},{5,4},{6,5},{7,6},{8,11},{9,8},{10,9... | collective-permute-start | bytes 368648 | tf_op jit(solution)/shard_map/ppermute | solution.py:217
  18.3 34.2 %collective-permute-start.46 = (bf16[12,5120]{1,0:T(8,128)(2,1)S(1)}, bf16[12,5120]{1,0:T(8,128)(2,1)S(1)}, u32[]{:S(2)}, u32[]{:S(2)}) collective-permute-start(bf16[12,5120]{1,0:T(8,128)(2,1)S(1)} %get-tuple-element.172), channel_id=1, source_target_pairs={{0,1},{1,2},{2,3},{3,0},{4,5},{5,6},{6,7},{7,4},{8,9},{9,10},{10,1... | collective-permute-start | bytes 368648 | tf_op jit(solution)/shard_map/ppermute | solution.py:217
  64.2 21.6 %collective-permute-start.13 = (bf16[4,48,1536]{2,1,0:T(8,128)(2,1)S(1)}, bf16[4,48,1536]{2,1,0:T(8,128)(2,1)S(1)}, u32[]{:S(2)}, u32[]{:S(2)}) collective-permute-start(bf16[4,48,1536]{2,1,0:T(8,128)(2,1)S(1)} %pad_maximum_fusion.2.refs_4_), channel_id=1, source_target_pairs={{0,12},{1,13},{2,14},{3,15},{4,0},{5,1},{6,2},{7,3},{8,4},{9,5},{1... | collective-permute-start | bytes 1769480 | tf_op jit(solution)/shard_map/ppermute | solution.py:217
  95.8 28.5 %collective-permute-start.26 = (bf16[16,4,48,192]{3,2,1,0:T(8,128)(2,1)}, bf16[16,4,48,192]{3,2,1,0:T(8,128)(2,1)}, u32[]{:S(2)}, u32[]{:S(2)}) collective-permute-start(bf16[16,4,48,192]{3,2,1,0:T(8,128)(2,1)} %get-tuple-element.76.refs_2_), channel_id=1, source_target_pairs={{0,64},{64,0},{1,65},{65,1},{2,66},{66,2},{3,67},{67,3},{4,68},{68... | collective-permute-start | bytes 3538952 | tf_op jit(solution)/shard_map/ppermute | solution.py:229
  99.3 25.0 %collective-permute-start.24 = (bf16[4,192,640]{2,1,0:T(8,128)(2,1)}, bf16[4,192,640]{2,1,0:T(8,128)(2,1)}, u32[]{:S(2)}, u32[]{:S(2)}) collective-permute-start(bf16[4,192,640]{2,1,0:T(8,128)(2,1)} %get-tuple-element.74.mine_ref.refs_0_), channel_id=1, source_target_pairs={{0,64},{64,0},{1,65},{65,1},{2,66},{66,2},{3,67},{67,3},{4,68},{68... | collective-permute-start | bytes 2949128 | tf_op jit(solution)/shard_map/ppermute | solution.py:229
  106.0 38.1 %collective-permute-start.52 = (bf16[192,5120]{1,0:T(8,128)(2,1)}, bf16[192,5120]{1,0:T(8,128)(2,1)}, u32[]{:S(2)}, u32[]{:S(2)}) collective-permute-start(bf16[192,5120]{1,0:T(8,128)(2,1)} %stack_rows.5.refs_0_), channel_id=1, source_target_pairs={{0,16},{1,17},{2,18},{3,19},{4,20},{5,21},{6,22},{7,23},{8,24},{9,... | collective-permute-start | bytes 5898248 | tf_op jit(solution)/shard_map/ppermute | solution.py:217
  106.7 42.6 %collective-permute-start.25 = (bf16[4,4,48,1536]{3,2,1,0:T(8,128)(2,1)S(1)}, bf16[4,4,48,1536]{3,2,1,0:T(8,128)(2,1)}, u32[]{:S(2)}, u32[]{:S(2)}) collective-permute-start(bf16[4,4,48,1536]{3,2,1,0:T(8,128)(2,1)S(1)} %copy-done.2), channel_id=1, source_target_pairs={{0,64},{64,0},{1,65},{65,1},{2,66},{66,2},{3,67},{67,3},{4,68},{68... | collective-permute-start | bytes 7077896 | tf_op jit(solution)/shard_map/ppermute | solution.py:229
  117.7 52.6 %collective-permute-start.53 = (bf16[192,5120]{1,0:T(8,128)(2,1)}, bf16[192,5120]{1,0:T(8,128)(2,1)}, u32[]{:S(2)}, u32[]{:S(2)}) collective-permute-start(bf16[192,5120]{1,0:T(8,128)(2,1)} %stack_rows.5.refs_0_), channel_id=1, source_target_pairs={{0,48},{1,49},{2,50},{3,51},{4,52},{5,53},{6,54},{7,55},{8,56},{9,... | collective-permute-start | bytes 5898248 | tf_op jit(solution)/shard_map/ppermute | solution.py:217
  124.3 46.0 %collective-permute-start.43 = (bf16[192,5120]{1,0:T(8,128)(2,1)}, bf16[192,5120]{1,0:T(8,128)(2,1)}, u32[]{:S(2)}, u32[]{:S(2)}) collective-permute-start(bf16[192,5120]{1,0:T(8,128)(2,1)} %stack_rows.4.refs_0_), channel_id=1, source_target_pairs={{0,4},{1,5},{2,6},{3,7},{4,8},{5,9},{6,10},{7,11},{8,12},{9,13},{1... | collective-permute-start | bytes 5898248 | tf_op jit(solution)/shard_map/ppermute | solution.py:217
  124.4 46.3 %collective-permute-start.34 = (bf16[192,5120]{1,0:T(8,128)(2,1)}, bf16[192,5120]{1,0:T(8,128)(2,1)}, u32[]{:S(2)}, u32[]{:S(2)}) collective-permute-start(bf16[192,5120]{1,0:T(8,128)(2,1)} %stack_rows.3.refs_0_), channel_id=1, source_target_pairs={{0,1},{1,2},{2,3},{3,0},{4,5},{5,6},{6,7},{7,4},{8,9},{9,10},{10,1... | collective-permute-start | bytes 5898248 | tf_op jit(solution)/shard_map/ppermute | solution.py:217
  144.1 40.9 %collective-permute-start.54 = (bf16[192,5120]{1,0:T(8,128)(2,1)}, bf16[192,5120]{1,0:T(8,128)(2,1)}, u32[]{:S(2)}, u32[]{:S(2)}) collective-permute-start(bf16[192,5120]{1,0:T(8,128)(2,1)} %collective-permute-done.52.refs_1_), channel_id=1, source_target_pairs={{0,16},{1,17},{2,18},{3,19},{4,20},{5,21},{6,22},{7,23},{8,24},{9,... | collective-permute-start | bytes 5898248 | tf_op jit(solution)/shard_map/ppermute | solution.py:217
  170.3 45.7 %collective-permute-start.44 = (bf16[192,5120]{1,0:T(8,128)(2,1)}, bf16[192,5120]{1,0:T(8,128)(2,1)}, u32[]{:S(2)}, u32[]{:S(2)}) collective-permute-start(bf16[192,5120]{1,0:T(8,128)(2,1)} %stack_rows.4.refs_0_), channel_id=1, source_target_pairs={{0,12},{1,13},{2,14},{3,15},{4,0},{5,1},{6,2},{7,3},{8,4},{9,5},{1... | collective-permute-start | bytes 5898248 | tf_op jit(solution)/shard_map/ppermute | solution.py:217
  170.4 53.4 %collective-permute-start.35 = (bf16[192,5120]{1,0:T(8,128)(2,1)S(1)}, bf16[192,5120]{1,0:T(8,128)(2,1)}, u32[]{:S(2)}, u32[]{:S(2)}) collective-permute-start(bf16[192,5120]{1,0:T(8,128)(2,1)S(1)} %copy-done.3), channel_id=1, source_target_pairs={{0,3},{1,0},{2,1},{3,2},{4,7},{5,4},{6,5},{7,6},{8,11},{9,8},{10,9... | collective-permute-start | bytes 5898248 | tf_op jit(solution)/shard_map/ppermute | solution.py:217
  170.7 46.4 %collective-permute-start.45 = (bf16[192,5120]{1,0:T(8,128)(2,1)}, bf16[192,5120]{1,0:T(8,128)(2,1)}, u32[]{:S(2)}, u32[]{:S(2)}) collective-permute-start(bf16[192,5120]{1,0:T(8,128)(2,1)} %collective-permute-done.43.refs_1_), channel_id=1, source_target_pairs={{0,4},{1,5},{2,6},{3,7},{4,8},{5,9},{6,10},{7,11},{8,12},{9,13},{1... | collective-permute-start | bytes 5898248 | tf_op jit(solution)/shard_map/ppermute | solution.py:217
  172.6 51.2 %collective-permute-start.36 = (bf16[192,5120]{1,0:T(8,128)(2,1)}, bf16[192,5120]{1,0:T(8,128)(2,1)}, u32[]{:S(2)}, u32[]{:S(2)}) collective-permute-start(bf16[192,5120]{1,0:T(8,128)(2,1)} %collective-permute-done.34.refs_1_), channel_id=1, source_target_pairs={{0,1},{1,2},{2,3},{3,0},{4,5},{5,6},{6,7},{7,4},{8,9},{9,10},{10,1... | collective-permute-start | bytes 5898248 | tf_op jit(solution)/shard_map/ppermute | solution.py:217
  185.0 127.7 %collective-permute-start.105 = (bf16[192,5120]{1,0:T(8,128)(2,1)}, bf16[192,5120]{1,0:T(8,128)(2,1)}, u32[]{:S(2)}, u32[]{:S(2)}) collective-permute-start(bf16[192,5120]{1,0:T(8,128)(2,1)} %get-tuple-element.131), channel_id=1, source_target_pairs={{0,1},{1,2},{2,3},{3,0},{4,5},{5,6},{6,7},{7,4},{8,9},{9,10},{10,1... | collective-permute-start | bytes 5898248 | tf_op jit(solution)/shard_map/ppermute | solution.py:217
  250.7 68.9 %collective-permute-start.96 = (bf16[192,5120]{1,0:T(8,128)(2,1)}, bf16[192,5120]{1,0:T(8,128)(2,1)}, u32[]{:S(2)}, u32[]{:S(2)}) collective-permute-start(bf16[192,5120]{1,0:T(8,128)(2,1)} %get-tuple-element.127), channel_id=1, source_target_pairs={{0,4},{1,5},{2,6},{3,7},{4,8},{5,9},{6,10},{7,11},{8,12},{9,13},{1... | collective-permute-start | bytes 5898248 | tf_op jit(solution)/shard_map/ppermute | solution.py:217
  250.7 70.2 %collective-permute-start.87 = (bf16[192,5120]{1,0:T(8,128)(2,1)}, bf16[192,5120]{1,0:T(8,128)(2,1)S(1)}, u32[]{:S(2)}, u32[]{:S(2)}) collective-permute-start(bf16[192,5120]{1,0:T(8,128)(2,1)} %get-tuple-element.123), channel_id=1, source_target_pairs={{0,16},{1,17},{2,18},{3,19},{4,20},{5,21},{6,22},{7,23},{8,24},{9,... | collective-permute-start | bytes 5898248 | tf_op jit(solution)/shard_map/ppermute | solution.py:217
  283.8 26.9 %collective-permute-start.56 = (bf16[128,384]{1,0:T(8,128)(2,1)S(1)}, bf16[128,384]{1,0:T(8,128)(2,1)S(1)}, u32[]{:S(2)}, u32[]{:S(2)}) collective-permute-start(bf16[128,384]{1,0:T(8,128)(2,1)S(1)} %constant_dynamic-slice_fusion), channel_id=1, source_target_pairs={{0,64},{64,0},{1,65},{65,1},{2,66},{66,2},{3,67},{67,3},{4,68},{68... | collective-permute-start | bytes 294920 | tf_op jit(solution)/shard_map/ppermute | solution.py:229
  289.9 59.2 %collective-permute-start.107 = (bf16[192,5120]{1,0:T(8,128)(2,1)}, bf16[192,5120]{1,0:T(8,128)(2,1)}, u32[]{:S(2)}, u32[]{:S(2)}) collective-permute-start(bf16[192,5120]{1,0:T(8,128)(2,1)} %get-tuple-element.132), channel_id=1, source_target_pairs={{0,3},{1,0},{2,1},{3,2},{4,7},{5,4},{6,5},{7,6},{8,11},{9,8},{10,9... | collective-permute-start | bytes 5898248 | tf_op jit(solution)/shard_map/ppermute | solution.py:217
  326.6 26.2 %collective-permute-start.106 = (bf16[192,5120]{1,0:T(8,128)(2,1)}, bf16[192,5120]{1,0:T(8,128)(2,1)}, u32[]{:S(2)}, u32[]{:S(2)}) collective-permute-start(bf16[192,5120]{1,0:T(8,128)(2,1)} %add_convert_fusion.1), channel_id=1, source_target_pairs={{0,1},{1,2},{2,3},{3,0},{4,5},{5,6},{6,7},{7,4},{8,9},{9,10},{10,1... | collective-permute-start | bytes 5898248 | tf_op jit(solution)/shard_map/ppermute | solution.py:217
  336.7 43.7 %collective-permute-start.98 = (bf16[192,5120]{1,0:T(8,128)(2,1)}, bf16[192,5120]{1,0:T(8,128)(2,1)}, u32[]{:S(2)}, u32[]{:S(2)}) collective-permute-start(bf16[192,5120]{1,0:T(8,128)(2,1)} %get-tuple-element.128), channel_id=1, source_target_pairs={{0,12},{1,13},{2,14},{3,15},{4,0},{5,1},{6,2},{7,3},{8,4},{9,5},{1... | collective-permute-start | bytes 5898248 | tf_op jit(solution)/shard_map/ppermute | solution.py:217
  336.9 50.5 %collective-permute-start.89 = (bf16[192,5120]{1,0:T(8,128)(2,1)}, bf16[192,5120]{1,0:T(8,128)(2,1)}, u32[]{:S(2)}, u32[]{:S(2)}) collective-permute-start(bf16[192,5120]{1,0:T(8,128)(2,1)} %get-tuple-element.124), channel_id=1, source_target_pairs={{0,48},{1,49},{2,50},{3,51},{4,52},{5,53},{6,54},{7,55},{8,56},{9,... | collective-permute-start | bytes 5898248 | tf_op jit(solution)/shard_map/ppermute | solution.py:217
  341.4 41.9 %collective-permute-start.97 = (bf16[192,5120]{1,0:T(8,128)(2,1)}, bf16[192,5120]{1,0:T(8,128)(2,1)}, u32[]{:S(2)}, u32[]{:S(2)}) collective-permute-start(bf16[192,5120]{1,0:T(8,128)(2,1)} %add_convert_fusion.3), channel_id=1, source_target_pairs={{0,4},{1,5},{2,6},{3,7},{4,8},{5,9},{6,10},{7,11},{8,12},{9,13},{1... | collective-permute-start | bytes 5898248 | tf_op jit(solution)/shard_map/ppermute | solution.py:217
  349.1 40.8 %collective-permute-start.88 = (bf16[192,5120]{1,0:T(8,128)(2,1)S(1)}, bf16[192,5120]{1,0:T(8,128)(2,1)S(1)}, u32[]{:S(2)}, u32[]{:S(2)}) collective-permute-start(bf16[192,5120]{1,0:T(8,128)(2,1)S(1)} %add_convert_fusion.5), channel_id=1, source_target_pairs={{0,16},{1,17},{2,18},{3,19},{4,20},{5,21},{6,22},{7,23},{8,24},{9,... | collective-permute-start | bytes 5898248 | tf_op jit(solution)/shard_map/ppermute | solution.py:217
  352.8 40.2 %collective-permute-start.63 = (bf16[192,640]{1,0:T(8,128)(2,1)}, bf16[192,640]{1,0:T(8,128)(2,1)S(1)}, u32[]{:S(2)}, u32[]{:S(2)}) collective-permute-start(bf16[192,640]{1,0:T(8,128)(2,1)} %get-tuple-element.111), channel_id=1, source_target_pairs={{0,16},{1,17},{2,18},{3,19},{4,20},{5,21},{6,22},{7,23},{8,24},{9,... | collective-permute-start | bytes 737288 | tf_op jit(solution)/shard_map/ppermute | solution.py:217
  387.5 22.5 %collective-permute-start.80 = (bf16[16,48,192]{2,1,0:T(8,128)(2,1)S(1)}, bf16[16,48,192]{2,1,0:T(8,128)(2,1)S(1)}, u32[]{:S(2)}, u32[]{:S(2)}) collective-permute-start(bf16[16,48,192]{2,1,0:T(8,128)(2,1)S(1)} %copy-done.50), channel_id=1, source_target_pairs={{0,3},{1,0},{2,1},{3,2},{4,7},{5,4},{6,5},{7,6},{8,11},{9,8},{10,9... | collective-permute-start | bytes 884744 | tf_op jit(solution)/shard_map/ppermute | solution.py:217
  389.9 23.6 %collective-permute-start.69 = (bf16[4,48,1536]{2,1,0:T(8,128)(2,1)S(1)}, bf16[4,48,1536]{2,1,0:T(8,128)(2,1)S(1)}, u32[]{:S(2)}, u32[]{:S(2)}) collective-permute-start(bf16[4,48,1536]{2,1,0:T(8,128)(2,1)S(1)} %copy-done.49), channel_id=1, source_target_pairs={{0,4},{1,5},{2,6},{3,7},{4,8},{5,9},{6,10},{7,11},{8,12},{9,13},{1... | collective-permute-start | bytes 1769480 | tf_op jit(solution)/shard_map/ppermute | solution.py:217
  394.0 73.8 %collective-permute-start.71 = (bf16[4,48,1536]{2,1,0:T(8,128)(2,1)S(1)}, bf16[4,48,1536]{2,1,0:T(8,128)(2,1)S(1)}, u32[]{:S(2)}, u32[]{:S(2)}) collective-permute-start(bf16[4,48,1536]{2,1,0:T(8,128)(2,1)S(1)} %copy-done.48), channel_id=1, source_target_pairs={{0,12},{1,13},{2,14},{3,15},{4,0},{5,1},{6,2},{7,3},{8,4},{9,5},{1... | collective-permute-start | bytes 1769480 | tf_op jit(solution)/shard_map/ppermute | solution.py:217
  410.0 39.4 %collective-permute-start.110 = (bf16[48,5120]{1,0:T(8,128)(2,1)S(1)}, bf16[48,5120]{1,0:T(8,128)(2,1)S(1)}, u32[]{:S(2)}, u32[]{:S(2)}) collective-permute-start(bf16[48,5120]{1,0:T(8,128)(2,1)S(1)} %get-tuple-element.159), channel_id=1, source_target_pairs={{0,48},{1,49},{2,50},{3,51},{4,52},{5,53},{6,54},{7,55},{8,56},{9,... | collective-permute-start | bytes 1474568 | tf_op jit(solution)/shard_map/ppermute | solution.py:217
  449.4 21.7 %collective-permute-start.70 = (bf16[4,48,1536]{2,1,0:T(8,128)(2,1)S(1)}, bf16[4,48,1536]{2,1,0:T(8,128)(2,1)S(1)}, u32[]{:S(2)}, u32[]{:S(2)}) collective-permute-start(bf16[4,48,1536]{2,1,0:T(8,128)(2,1)S(1)} %add_convert_fusion.7), channel_id=1, source_target_pairs={{0,4},{1,5},{2,6},{3,7},{4,8},{5,9},{6,10},{7,11},{8,12},{9,13},{1... | collective-permute-start | bytes 1769480 | tf_op jit(solution)/shard_map/ppermute | solution.py:217
  471.3 23.1 %collective-permute-start.95 = (bf16[12,5120]{1,0:T(8,128)(2,1)S(1)}, bf16[12,5120]{1,0:T(8,128)(2,1)S(1)}, u32[]{:S(2)}, u32[]{:S(2)}) collective-permute-start(bf16[12,5120]{1,0:T(8,128)(2,1)S(1)} %get-tuple-element.167), channel_id=1, source_target_pairs={{0,3},{1,0},{2,1},{3,2},{4,7},{5,4},{6,5},{7,6},{8,11},{9,8},{10,9... | collective-permute-start | bytes 368648 | tf_op jit(solution)/shard_map/ppermute | solution.py:217
  (135 other events, 1594.1 us)
